TPU v7x, 256 devices: a whole 4x4x8 slice. The times are simulated.
256 devices in a mesh: ctx: 64 (over z, x, y_lo), head: 4 (over y_hi, core).
Axes of the slice: x: 4, y: 4 (y_hi: 2, y_lo: 2; y = y_hi * 2 + y_lo), z: 8, core: 2. Of those that a mesh axis runs over, the one named last changes fastest.
Arguments:
- query: float32 [8192, 1536], P('ctx', 'head'), may hold values from -240 to 240
- key: float32 [8192, 1536], P('ctx', 'head'), may hold values from -6 to 6
- value: float32 [8192, 1536], P('ctx', 'head'), may hold values from -6 to 6
- segment: int32 [8192], P('ctx'), may hold values from 0 to 31, never falling along the last dimension, each value on 1 to 768 neighbouring positions
- band: int32 [16], replicated, may hold values from 1 to 3, as said below
- out_weight: float32 [1536, 1536], P('head'), may hold values from -0.15625 to 0.15625
- cotangent: float32 [8192, 1536], P('ctx', 'head'), may hold values from -16 to 16
Outputs:
- output: float32 [8192, 1536], P('ctx', 'head')
- grad_query: float32 [8192, 1536], P('ctx', 'head')
- grad_key: float32 [8192, 1536], P('ctx', 'head')
- grad_value: float32 [8192, 1536], P('ctx', 'head')
- grad_weight: float32 [1536, 1536], P('head', 'ctx')
Inputs may be any that keep to these rules, and one draw needn't show every extreme that they name: A head attends to keys at most band blocks from the query's block; some head has band 3. `segment`: utterance numbers never fall along the frames.
All inputs are finite; a program needn't handle non-finite values.
Results may differ from a plain program's by a relative error of at most 0.0003.
Values sent between devices are 32-bit elements; how exact they have to be, the bound alone decides.
A program may use at most 64 MiB of HBM per device.

v0:
```python
import math

import jax
import jax.numpy as jnp
from jax import lax
from jax.sharding import PartitionSpec as P

HEAD_DIM = 96
REACH = 3


def passed_along(block, axis, distance):
    devices = range(lax.axis_size(axis))
    route = [(i - distance, i) for i in devices if i - distance in devices]
    return lax.ppermute(block, axis, route)


def shards(query, key, value, segment, band, out_weight, cotangent):
    frame_rows = query.shape[0]
    local_width = query.shape[1]
    local_heads = local_width // HEAD_DIM
    scale = 1.0 / math.sqrt(HEAD_DIM)
    highest = lax.Precision.HIGHEST
    first_head = lax.axis_index("head") * local_heads
    band_here = lax.dynamic_slice_in_dim(band, first_head, local_heads, 0)
    labels = (segment + 1).astype(jnp.float32)

    def shaped(values):
        return values.reshape(frame_rows, local_heads, HEAD_DIM)

    query_heads = shaped(query)
    tiles = {0: (key, value, labels)}
    above = tiles[0]
    below = tiles[0]
    for distance in range(1, REACH + 1):
        above = passed_along((above[0], above[1], above[2]), "ctx", -1)
        below = passed_along((below[0], below[1], below[2]), "ctx", 1)
        tiles[distance] = above
        tiles[-distance] = below
    order = [0]
    for distance in range(1, REACH + 1):
        order = order + [distance, -distance]

    def permitted(offset, tile_labels):
        same = (labels[:, None] == tile_labels[None, :])[None, :, :]
        return same & (abs(offset) <= band_here)[:, None, None]

    def tile_scores(keys_tile, allowed):
        scores = (
            jnp.einsum("ihe,jhe->hij", query_heads, shaped(keys_tile), precision=highest) * scale
        )
        return jnp.where(allowed, scores, -1e30)

    state = (
        jnp.full((local_heads, frame_rows), -1e30, jnp.float32),
        jnp.zeros((local_heads, frame_rows), jnp.float32),
        jnp.zeros((frame_rows, local_heads, HEAD_DIM), jnp.float32),
    )
    for offset in order:
        keys_tile, values_tile, tile_labels = tiles[offset]
        allowed = permitted(offset, tile_labels)
        advance_largest, advance_total, advance_gathered = state
        advance_scores = tile_scores(keys_tile, allowed)
        top = jnp.maximum(advance_largest, jnp.max(advance_scores, axis=2))
        carry_factor = jnp.exp(advance_largest - top)
        weights = jnp.where(allowed, jnp.exp(advance_scores - top[:, :, None]), 0.0)
        advance_total = advance_total * carry_factor + jnp.sum(weights, axis=2)
        advance_gathered = advance_gathered * carry_factor.T[:, :, None] + jnp.einsum(
            "hij,jhe->ihe", weights, shaped(values_tile), precision=highest
        )
        state = (top, advance_total, advance_gathered)
    largest, total, gathered = state
    attended_heads = gathered / total.T[:, :, None]
    attended = attended_heads.reshape(frame_rows, local_width)
    log_total = largest + jnp.log(total)
    partial_out = jnp.dot(attended, out_weight, precision=highest)
    output = lax.psum_scatter(partial_out, "head", scatter_dimension=1, tiled=True)
    piece = lax.all_gather(cotangent, "head", axis=1, tiled=True)
    grad_part = jnp.dot(piece, out_weight.T, precision=highest)
    weight_part = jnp.dot(attended.T, piece, precision=highest)
    grad_weight = lax.psum_scatter(weight_part, "ctx", scatter_dimension=1, tiled=True)
    grad_heads = shaped(grad_part)
    delta = jnp.sum(grad_heads * attended_heads, axis=2).T
    grad_query = jnp.zeros((frame_rows, local_heads, HEAD_DIM), jnp.float32)
    parts = {}
    for offset in order:
        keys_tile, values_tile, tile_labels = tiles[offset]
        allowed = permitted(offset, tile_labels)
        retreat_scores = tile_scores(keys_tile, allowed)
        probs = jnp.where(allowed, jnp.exp(retreat_scores - log_total[:, :, None]), 0.0)
        value_part = jnp.einsum("hij,ihe->jhe", probs, grad_heads, precision=highest)
        grad_probs = jnp.einsum("ihe,jhe->hij", grad_heads, shaped(values_tile), precision=highest)
        grad_scores = probs * (grad_probs - delta[:, :, None])
        query_part = scale * jnp.einsum(
            "hij,jhe->ihe", grad_scores, shaped(keys_tile), precision=highest
        )
        key_part = scale * jnp.einsum("hij,ihe->jhe", grad_scores, query_heads, precision=highest)
        grad_query = grad_query + query_part
        parts[offset] = (
            key_part.reshape(frame_rows, local_width),
            value_part.reshape(frame_rows, local_width),
        )
    grad_keys, grad_values = parts[0]
    blank = jnp.zeros((frame_rows, local_width), jnp.float32)
    toward_above = (blank, blank)
    toward_below = (blank, blank)
    for distance in range(REACH, 0, -1):
        toward_above = passed_along(
            (toward_above[0] + parts[distance][0], toward_above[1] + parts[distance][1]), "ctx", 1
        )
        toward_below = passed_along(
            (toward_below[0] + parts[-distance][0], toward_below[1] + parts[-distance][1]),
            "ctx",
            -1,
        )
    grad_keys = grad_keys + toward_above[0] + toward_below[0]
    grad_values = grad_values + toward_above[1] + toward_below[1]
    return (
        output,
        grad_query.reshape(frame_rows, local_width),
        grad_keys,
        grad_values,
        grad_weight,
    )


def solution(mesh):
    in_specs = (
        P("ctx", "head"),
        P("ctx", "head"),
        P("ctx", "head"),
        P("ctx"),
        P(),
        P("head", None),
        P("ctx", "head"),
    )
    out_specs = (
        P("ctx", "head"),
        P("ctx", "head"),
        P("ctx", "head"),
        P("ctx", "head"),
        P("head", "ctx"),
    )
    return jax.shard_map(shards, mesh=mesh, in_specs=in_specs, out_specs=out_specs, check_vma=False)
```

profile of v0, /device:TPU:8, one launch (start us, length us, event | category | flops | bytes accessed | tf_op | source)
XLA Modules:
  0.0 538.7 jit_solution(15389981083796034002)
XLA Ops:
  8.1 4.1 collective-permute-start
  12.1 2.6 collective-permute-start.3
  17.2 4.1 collective-permute-start.1
  21.3 2.6 collective-permute-start.5
  24.0 9.9 %all_gather.3 = f32[128,1536]{1,0:T(8,128)S(1)} all-gather(f32[128,384]{1,0:T(8,128)} %param.13), channel_id=1, replica_groups=mesh['ctx'=64,'head'=4] {'head'}, dimensions={1}, use_global_device_ids=true | all-gather | bytes 983040 | tf_op jit(solution)/shard_map/all_gather | solution.py:78
  35.9 7.5 %collective-permute-start.6 = (f32[128]{0:T(128)S(1)}, f32[128]{0:T(128)S(1)}, u32[]{:S(2)}, u32[]{:S(2)}) collective-permute-start(f32[128]{0:T(128)S(1)} %collective-permute-done), channel_id=1, source_target_pairs={{4,0},{8,4},{12,8},{16,12},{20,16},{24,20},{28,24},{32,28},{36,32}... | collective-permute-start | bytes 1544 | tf_op jit(solution)/shard_map/ppermute | solution.py:15
  43.4 2.8 collective-permute-start.9
  47.5 3.5 collective-permute-start.12
  51.1 3.2 collective-permute-start.15
  58.5 3.2 collective-permute-start.2
  63.9 2.8 fusion.135
  68.4 3.6 collective-permute-start.10
  73.7 2.9 collective-permute-start.7
  78.4 3.8 collective-permute-start.11
  82.2 2.8 fusion.134
  86.8 2.7 collective-permute-start.8
  89.5 2.8 fusion.133
  94.1 4.0 collective-permute-start.16
  99.8 2.5 collective-permute-start.13
  104.1 4.2 collective-permute-start.17
  108.3 2.8 fusion.132
  115.4 2.8 fusion.131
  119.9 2.8 fusion.130
  165.3 3.5 fusion.141
  211.9 4.6 collective-permute-start.18
  220.3 5.1 collective-permute-start.24
  231.3 3.9 collective-permute-start.19
  241.0 7.2 %collective-permute-start.25 = (f32[128,384]{1,0:T(8,128)}, f32[128,384]{1,0:T(8,128)}, u32[]{:S(2)}, u32[]{:S(2)}) collective-permute-start(f32[128,384]{1,0:T(8,128)} %add.208), channel_id=1, source_target_pairs={{0,4},{4,8},{8,12},{12,16},{16,20},{20,24},{24,28},{28,32},{32,36}... | collective-permute-start | bytes 589832 | tf_op jit(solution)/shard_map/ppermute | solution.py:15
  249.0 6.0 %collective-permute-start.20 = (f32[128,384]{1,0:T(8,128)}, f32[128,384]{1,0:T(8,128)}, u32[]{:S(2)}, u32[]{:S(2)}) collective-permute-start(f32[128,384]{1,0:T(8,128)} %add.203), channel_id=1, source_target_pairs={{0,4},{4,8},{8,12},{12,16},{16,20},{20,24},{24,28},{28,32},{32,36}... | collective-permute-start | bytes 589832 | tf_op jit(solution)/shard_map/ppermute | solution.py:15
  262.7 9.2 %collective-permute-start.26 = (f32[128,384]{1,0:T(8,128)S(1)}, f32[128,384]{1,0:T(8,128)S(1)}, u32[]{:S(2)}, u32[]{:S(2)}) collective-permute-start(f32[128,384]{1,0:T(8,128)S(1)} %add.209), channel_id=1, source_target_pairs={{0,4},{4,8},{8,12},{12,16},{16,20},{20,24},{24,28},{28,32},{32,36}... | collective-permute-start | bytes 589832 | tf_op jit(solution)/shard_map/ppermute | solution.py:15
  273.7 2.7 collective-permute-done.26
  277.1 254.7 %reduce-scatter.8.cloned.1.call-done = f32[384,24]{0,1:T(8,128)} async-done(((f32[384,1536]{0,1:T(8,128)}), f32[384,24]{0,1:T(8,128)}) %reduce-scatter.8.cloned.1.call-update) | async-done | bytes 36880
  (284 shorter events, 142.0 us)
Async XLA Ops:
  7.2 269.9 %reduce-scatter.6.cloned.1.call-start = ((), (), s32[]{:S(2)}) async-start(), calls=%async_computation.2 | async-start | bytes 983040 | tf_op jit(solution)/shard_map/reduce_scatter | solution.py:77
  8.1 27.8 %collective-permute-start = (f32[128]{0:T(128)S(1)}, f32[128]{0:T(128)S(1)}, u32[]{:S(2)}, u32[]{:S(2)}) collective-permute-start(f32[128]{0:T(128)S(1)} %add_convert_fusion), channel_id=1, source_target_pairs={{4,0},{8,4},{12,8},{16,12},{20,16},{24,20},{28,24},{32,28},{36,32}... | collective-permute-start | bytes 1544 | tf_op jit(solution)/shard_map/ppermute | solution.py:15
  12.1 31.2 %collective-permute-start.3 = (f32[128]{0:T(128)S(1)}, f32[128]{0:T(128)S(1)}, u32[]{:S(2)}, u32[]{:S(2)}) collective-permute-start(f32[128]{0:T(128)S(1)} %add_convert_fusion), channel_id=1, source_target_pairs={{0,4},{4,8},{8,12},{12,16},{16,20},{20,24},{24,28},{28,32},{32,36}... | collective-permute-start | bytes 1544 | tf_op jit(solution)/shard_map/ppermute | solution.py:15
  14.8 51.9 %collective-permute-start.4 = (f32[128,384]{1,0:T(8,128)}, f32[128,384]{1,0:T(8,128)}, u32[]{:S(2)}, u32[]{:S(2)}) collective-permute-start(f32[128,384]{1,0:T(8,128)} %param.8), channel_id=1, source_target_pairs={{0,4},{4,8},{8,12},{12,16},{16,20},{20,24},{24,28},{28,32},{32,36}... | collective-permute-start | bytes 589832 | tf_op jit(solution)/shard_map/ppermute | solution.py:15
  17.2 54.8 %collective-permute-start.1 = (f32[128,384]{1,0:T(8,128)}, f32[128,384]{1,0:T(8,128)}, u32[]{:S(2)}, u32[]{:S(2)}) collective-permute-start(f32[128,384]{1,0:T(8,128)} %param.8), channel_id=1, source_target_pairs={{4,0},{8,4},{12,8},{16,12},{20,16},{24,20},{28,24},{32,28},{36,32}... | collective-permute-start | bytes 589832 | tf_op jit(solution)/shard_map/ppermute | solution.py:15
  21.3 55.3 %collective-permute-start.5 = (f32[128,384]{1,0:T(8,128)}, f32[128,384]{1,0:T(8,128)}, u32[]{:S(2)}, u32[]{:S(2)}) collective-permute-start(f32[128,384]{1,0:T(8,128)} %param.9), channel_id=1, source_target_pairs={{0,4},{4,8},{8,12},{12,16},{16,20},{20,24},{24,28},{28,32},{32,36}... | collective-permute-start | bytes 589832 | tf_op jit(solution)/shard_map/ppermute | solution.py:15
  35.9 11.6 %collective-permute-start.6 = (f32[128]{0:T(128)S(1)}, f32[128]{0:T(128)S(1)}, u32[]{:S(2)}, u32[]{:S(2)}) collective-permute-start(f32[128]{0:T(128)S(1)} %collective-permute-done), channel_id=1, source_target_pairs={{4,0},{8,4},{12,8},{16,12},{20,16},{24,20},{28,24},{32,28},{36,32}... | collective-permute-start | bytes 1544 | tf_op jit(solution)/shard_map/ppermute | solution.py:15
  43.4 7.7 %collective-permute-start.9 = (f32[128]{0:T(128)S(1)}, f32[128]{0:T(128)}, u32[]{:S(2)}, u32[]{:S(2)}) collective-permute-start(f32[128]{0:T(128)S(1)} %collective-permute-done.3), channel_id=1, source_target_pairs={{0,4},{4,8},{8,12},{12,16},{16,20},{20,24},{24,28},{28,32},{32,36}... | collective-permute-start | bytes 1544 | tf_op jit(solution)/shard_map/ppermute | solution.py:15
  47.5 11.0 %collective-permute-start.12 = (f32[128]{0:T(128)S(1)}, f32[128]{0:T(128)}, u32[]{:S(2)}, u32[]{:S(2)}) collective-permute-start(f32[128]{0:T(128)S(1)} %collective-permute-done.6), channel_id=1, source_target_pairs={{4,0},{8,4},{12,8},{16,12},{20,16},{24,20},{28,24},{32,28},{36,32}... | collective-permute-start | bytes 1544 | tf_op jit(solution)/shard_map/ppermute | solution.py:15
  51.1 10.7 %collective-permute-start.15 = (f32[128]{0:T(128)}, f32[128]{0:T(128)}, u32[]{:S(2)}, u32[]{:S(2)}) collective-permute-start(f32[128]{0:T(128)} %collective-permute-done.9), channel_id=1, source_target_pairs={{0,4},{4,8},{8,12},{12,16},{16,20},{20,24},{24,28},{28,32},{32,36}... | collective-permute-start | bytes 1544 | tf_op jit(solution)/shard_map/ppermute | solution.py:15
  58.5 26.6 %collective-permute-start.2 = (f32[128,384]{1,0:T(8,128)}, f32[128,384]{1,0:T(8,128)}, u32[]{:S(2)}, u32[]{:S(2)}) collective-permute-start(f32[128,384]{1,0:T(8,128)} %param.9), channel_id=1, source_target_pairs={{4,0},{8,4},{12,8},{16,12},{20,16},{24,20},{28,24},{32,28},{36,32}... | collective-permute-start | bytes 589832 | tf_op jit(solution)/shard_map/ppermute | solution.py:15
  68.4 23.9 %collective-permute-start.10 = (f32[128,384]{1,0:T(8,128)}, f32[128,384]{1,0:T(8,128)}, u32[]{:S(2)}, u32[]{:S(2)}) collective-permute-start(f32[128,384]{1,0:T(8,128)} %collective-permute-done.4), channel_id=1, source_target_pairs={{0,4},{4,8},{8,12},{12,16},{16,20},{20,24},{24,28},{28,32},{32,36}... | collective-permute-start | bytes 589832 | tf_op jit(solution)/shard_map/ppermute | solution.py:15
  73.7 24.4 %collective-permute-start.7 = (f32[128,384]{1,0:T(8,128)}, f32[128,384]{1,0:T(8,128)}, u32[]{:S(2)}, u32[]{:S(2)}) collective-permute-start(f32[128,384]{1,0:T(8,128)} %collective-permute-done.1), channel_id=1, source_target_pairs={{4,0},{8,4},{12,8},{16,12},{20,16},{24,20},{28,24},{32,28},{36,32}... | collective-permute-start | bytes 589832 | tf_op jit(solution)/shard_map/ppermute | solution.py:15
  78.4 23.9 %collective-permute-start.11 = (f32[128,384]{1,0:T(8,128)}, f32[128,384]{1,0:T(8,128)}, u32[]{:S(2)}, u32[]{:S(2)}) collective-permute-start(f32[128,384]{1,0:T(8,128)} %collective-permute-done.5), channel_id=1, source_target_pairs={{0,4},{4,8},{8,12},{12,16},{16,20},{20,24},{24,28},{28,32},{32,36}... | collective-permute-start | bytes 589832 | tf_op jit(solution)/shard_map/ppermute | solution.py:15
  86.8 24.4 %collective-permute-start.8 = (f32[128,384]{1,0:T(8,128)}, f32[128,384]{1,0:T(8,128)}, u32[]{:S(2)}, u32[]{:S(2)}) collective-permute-start(f32[128,384]{1,0:T(8,128)} %collective-permute-done.2), channel_id=1, source_target_pairs={{4,0},{8,4},{12,8},{16,12},{20,16},{24,20},{28,24},{32,28},{36,32}... | collective-permute-start | bytes 589832 | tf_op jit(solution)/shard_map/ppermute | solution.py:15
  94.1 28.7 %collective-permute-start.16 = (f32[128,384]{1,0:T(8,128)}, f32[128,384]{1,0:T(8,128)}, u32[]{:S(2)}, u32[]{:S(2)}) collective-permute-start(f32[128,384]{1,0:T(8,128)} %collective-permute-done.10), channel_id=1, source_target_pairs={{0,4},{4,8},{8,12},{12,16},{16,20},{20,24},{24,28},{28,32},{32,36}... | collective-permute-start | bytes 589832 | tf_op jit(solution)/shard_map/ppermute | solution.py:15
  99.8 18.3 %collective-permute-start.13 = (f32[128,384]{1,0:T(8,128)}, f32[128,384]{1,0:T(8,128)}, u32[]{:S(2)}, u32[]{:S(2)}) collective-permute-start(f32[128,384]{1,0:T(8,128)} %collective-permute-done.7), channel_id=1, source_target_pairs={{4,0},{8,4},{12,8},{16,12},{20,16},{24,20},{28,24},{32,28},{36,32}... | collective-permute-start | bytes 589832 | tf_op jit(solution)/shard_map/ppermute | solution.py:15
  104.1 39.9 %collective-permute-start.17 = (f32[128,384]{1,0:T(8,128)}, f32[128,384]{1,0:T(8,128)}, u32[]{:S(2)}, u32[]{:S(2)}) collective-permute-start(f32[128,384]{1,0:T(8,128)} %collective-permute-done.11), channel_id=1, source_target_pairs={{0,4},{4,8},{8,12},{12,16},{16,20},{20,24},{24,28},{28,32},{32,36}... | collective-permute-start | bytes 589832 | tf_op jit(solution)/shard_map/ppermute | solution.py:15
  112.9 24.7 %collective-permute-start.14 = (f32[128,384]{1,0:T(8,128)}, f32[128,384]{1,0:T(8,128)}, u32[]{:S(2)}, u32[]{:S(2)}) collective-permute-start(f32[128,384]{1,0:T(8,128)} %collective-permute-done.8), channel_id=1, source_target_pairs={{4,0},{8,4},{12,8},{16,12},{20,16},{24,20},{28,24},{32,28},{36,32}... | collective-permute-start | bytes 589832 | tf_op jit(solution)/shard_map/ppermute | solution.py:15
  152.7 379.1 %reduce-scatter.8.cloned.1.call-start = ((), (), s32[]{:S(2)}) async-start(), calls=%async_computation.3 | async-start | bytes 2396160
  211.9 19.4 %collective-permute-start.18 = (f32[128,384]{1,0:T(8,128)}, f32[128,384]{1,0:T(8,128)S(1)}, u32[]{:S(2)}, u32[]{:S(2)}) collective-permute-start(f32[128,384]{1,0:T(8,128)} %copy.198), channel_id=1, source_target_pairs={{0,4},{4,8},{8,12},{12,16},{16,20},{20,24},{24,28},{28,32},{32,36}... | collective-permute-start | bytes 589832 | tf_op jit(solution)/shard_map/ppermute | solution.py:15
  216.5 18.8 %collective-permute-start.21 = (f32[128,384]{1,0:T(8,128)}, f32[128,384]{1,0:T(8,128)S(1)}, u32[]{:S(2)}, u32[]{:S(2)}) collective-permute-start(f32[128,384]{1,0:T(8,128)} %copy.205), channel_id=1, source_target_pairs={{4,0},{8,4},{12,8},{16,12},{20,16},{24,20},{28,24},{32,28},{36,32}... | collective-permute-start | bytes 589832 | tf_op jit(solution)/shard_map/ppermute | solution.py:15
  218.4 19.2 %collective-permute-start.27 = (f32[128,384]{1,0:T(8,128)}, f32[128,384]{1,0:T(8,128)S(1)}, u32[]{:S(2)}, u32[]{:S(2)}) collective-permute-start(f32[128,384]{1,0:T(8,128)} %copy.219), channel_id=1, source_target_pairs={{4,0},{8,4},{12,8},{16,12},{20,16},{24,20},{28,24},{32,28},{36,32}... | collective-permute-start | bytes 589832 | tf_op jit(solution)/shard_map/ppermute | solution.py:15
  220.3 19.9 %collective-permute-start.24 = (f32[128,384]{1,0:T(8,128)}, f32[128,384]{1,0:T(8,128)S(1)}, u32[]{:S(2)}, u32[]{:S(2)}) collective-permute-start(f32[128,384]{1,0:T(8,128)} %copy.212), channel_id=1, source_target_pairs={{0,4},{4,8},{8,12},{12,16},{16,20},{20,24},{24,28},{28,32},{32,36}... | collective-permute-start | bytes 589832 | tf_op jit(solution)/shard_map/ppermute | solution.py:15
  231.3 16.9 %collective-permute-start.19 = (f32[128,384]{1,0:T(8,128)S(1)}, f32[128,384]{1,0:T(8,128)S(1)}, u32[]{:S(2)}, u32[]{:S(2)}) collective-permute-start(f32[128,384]{1,0:T(8,128)S(1)} %add.202), channel_id=1, source_target_pairs={{0,4},{4,8},{8,12},{12,16},{16,20},{20,24},{24,28},{28,32},{32,36}... | collective-permute-start | bytes 589832 | tf_op jit(solution)/shard_map/ppermute | solution.py:15
  235.3 19.7 %collective-permute-start.22 = (f32[128,384]{1,0:T(8,128)S(1)}, f32[128,384]{1,0:T(8,128)S(1)}, u32[]{:S(2)}, u32[]{:S(2)}) collective-permute-start(f32[128,384]{1,0:T(8,128)S(1)} %add.205), channel_id=1, source_target_pairs={{4,0},{8,4},{12,8},{16,12},{20,16},{24,20},{28,24},{32,28},{36,32}... | collective-permute-start | bytes 589832 | tf_op jit(solution)/shard_map/ppermute | solution.py:15
  238.3 20.4 %collective-permute-start.28 = (f32[128,384]{1,0:T(8,128)}, f32[128,384]{1,0:T(8,128)}, u32[]{:S(2)}, u32[]{:S(2)}) collective-permute-start(f32[128,384]{1,0:T(8,128)} %add.211), channel_id=1, source_target_pairs={{4,0},{8,4},{12,8},{16,12},{20,16},{24,20},{28,24},{32,28},{36,32}... | collective-permute-start | bytes 589832 | tf_op jit(solution)/shard_map/ppermute | solution.py:15
  241.0 20.8 %collective-permute-start.25 = (f32[128,384]{1,0:T(8,128)}, f32[128,384]{1,0:T(8,128)}, u32[]{:S(2)}, u32[]{:S(2)}) collective-permute-start(f32[128,384]{1,0:T(8,128)} %add.208), channel_id=1, source_target_pairs={{0,4},{4,8},{8,12},{12,16},{16,20},{20,24},{24,28},{28,32},{32,36}... | collective-permute-start | bytes 589832 | tf_op jit(solution)/shard_map/ppermute | solution.py:15
  249.0 23.0 %collective-permute-start.20 = (f32[128,384]{1,0:T(8,128)}, f32[128,384]{1,0:T(8,128)}, u32[]{:S(2)}, u32[]{:S(2)}) collective-permute-start(f32[128,384]{1,0:T(8,128)} %add.203), channel_id=1, source_target_pairs={{0,4},{4,8},{8,12},{12,16},{16,20},{20,24},{24,28},{28,32},{32,36}... | collective-permute-start | bytes 589832 | tf_op jit(solution)/shard_map/ppermute | solution.py:15
  255.7 16.3 %collective-permute-start.23 = (f32[128,384]{1,0:T(8,128)}, f32[128,384]{1,0:T(8,128)}, u32[]{:S(2)}, u32[]{:S(2)}) collective-permute-start(f32[128,384]{1,0:T(8,128)} %add.206), channel_id=1, source_target_pairs={{4,0},{8,4},{12,8},{16,12},{20,16},{24,20},{28,24},{32,28},{36,32}... | collective-permute-start | bytes 589832 | tf_op jit(solution)/shard_map/ppermute | solution.py:15
  259.8 13.9 %collective-permute-start.29 = (f32[128,384]{1,0:T(8,128)S(1)}, f32[128,384]{1,0:T(8,128)S(1)}, u32[]{:S(2)}, u32[]{:S(2)}) collective-permute-start(f32[128,384]{1,0:T(8,128)S(1)} %add.212), channel_id=1, source_target_pairs={{4,0},{8,4},{12,8},{16,12},{20,16},{24,20},{28,24},{32,28},{36,32}... | collective-permute-start | bytes 589832 | tf_op jit(solution)/shard_map/ppermute | solution.py:15
  262.7 13.7 %collective-permute-start.26 = (f32[128,384]{1,0:T(8,128)S(1)}, f32[128,384]{1,0:T(8,128)S(1)}, u32[]{:S(2)}, u32[]{:S(2)}) collective-permute-start(f32[128,384]{1,0:T(8,128)S(1)} %add.209), channel_id=1, source_target_pairs={{0,4},{4,8},{8,12},{12,16},{16,20},{20,24},{24,28},{28,32},{32,36}... | collective-permute-start | bytes 589832 | tf_op jit(solution)/shard_map/ppermute | solution.py:15
  (77 other events, 963.3 us)
Sparse Core Ops, SparseCore 0:
  152.8 59.1 reduce-scatter.5
  215.2 316.5 reduce-scatter.7
where the time goes:
time: 546 us; the launch traced here: 539 us
  waiting for transfers between devices  258 us (47%)
  starting transfers between devices  110 us (20%)
  matrix products  75 us (14%)
  local copies, waits for them, and re-layouts  54 us (10%)
  other arithmetic  16.7 us (3%)
  between operations  15.4 us (3%)
  blocking collectives  9.91 us (2%)
    unnamed x3, waiting for transfers between devices  255 us
    ppermute x30, starting transfers between devices, passed_along(): return lax.ppermute(block, axis, route)  110 us
    ppermute x12, local copies, waits for them, and re-layouts, passed_along(): return lax.ppermute(block, axis, route)  20.8 us
    dot_general x7, matrix products, tile_scores(): jnp.einsum('ihe,jhe->hij', query_heads, shaped(keys_tile), precision=high...  18.6 us
    dot_general x7, matrix products, shards(): jnp.einsum('hij,ihe->jhe', probs, grad_heads, precision=highest)  13.6 us
    reshape x7, local copies, waits for them, and re-layouts, shards(): key_part.reshape(frame_rows, local_width)  12.3 us
    dot_general x7, matrix products, shards(): jnp.einsum('ihe,jhe->hij', grad_heads, shaped(values_tile), precision=hig...  11.5 us
    reshape x7, local copies, waits for them, and re-layouts, shards(): value_part.reshape(frame_rows, local_width)  11.3 us
  transfers between devices with their start and end apart: 32, of which 2 were waited for; matrix products, arithmetic and copies ran while one was open for 24% of the time, Pallas kernels for 0%

commit v1 on v0

v1 whole, which is shorter than its diff:
```python
import math

import jax
import jax.numpy as jnp
from jax import lax
from jax.experimental import pallas as pl
from jax.experimental.pallas import tpu as pltpu
from jax.sharding import PartitionSpec as P

MESH = pl.DeviceIdType.MESH
F32 = jnp.float32
BF16 = jnp.bfloat16
HD = 96
SCALE = 1.0 / math.sqrt(HD)
B = 128
W8 = 8 * B
NZ, NX = 8, 4
CHUNK = 32


def split2(x):
    hi = x.astype(BF16)
    return hi, (x - hi.astype(F32)).astype(BF16)


def split3(x):
    hi = x.astype(BF16)
    rest = x - hi.astype(F32)
    mid = rest.astype(BF16)
    return hi, mid, (rest - mid.astype(F32)).astype(BF16)


def dot(a, b):
    return jnp.dot(a, b, preferred_element_type=F32)


def dot_nt(a, b):
    return lax.dot_general(a, b, (((1,), (1,)), ((), ())), preferred_element_type=F32)


def pad_rows(x):
    return jnp.concatenate([x, jnp.zeros((B - HD, x.shape[1]), x.dtype)], axis=0)


def mul6(left, right):
    lh, lm, ll = split3(left)
    rh, rm, rl = split3(right)
    return dot(
        jnp.concatenate([lh, lh, lm, lm, lh, ll], axis=1),
        jnp.concatenate([rh, rm, rh, rm, rl, rh], axis=0),
    )


def mul4(left, right):
    lh, lm = split2(left)
    rh, rm = split2(right)
    return dot(
        jnp.concatenate([lh, lh, lm, lm], axis=1),
        jnp.concatenate([rh, rm, rh, rm], axis=0),
    )


def mul_window(hi, mid, right):
    rh, rm = split2(right)
    both = jnp.concatenate([rh, rm], axis=0)
    out = dot_nt(hi, both) + dot_nt(mid, both)
    return out[:, :B] + out[:, B:]


def mul3(lh, lm, rh, rm):
    return dot(lh, rh) + (dot(lh, rm) + dot(lm, rh))


def kernel(
    q_ref, k_ref, v_ref, seg_ref, band_ref, w_ref, cot_ref,
    out_ref, gq_ref, gk_ref, gv_ref, gw_ref,
    tq, tkv, kvs, kvw, qs, qw, dow, stw, cotw, wv, lab_col, lab_row,
    coth, cotm, cotth, cottm, wh, wm,
    s_ref, e_ref, dp_ref, ph, pm, col_ref, att_t, do_t, ath, atm,
    po, por, ps, pr, mx, xr, xs, zr, gsum, yr, gown, gsend, grecv,
    ss, kv_sem, q_sem, do_sem, st_sem, cot_sem, y_sem, po_sem, pr_sem, x_sem, z_sem, g_sem, w_sem,
):
    ctx = lax.axis_index("ctx")
    head = lax.axis_index("head")
    yl = ctx % 2
    pair_index = ctx // 2
    z, x = pair_index // NX, pair_index % NX
    core = head % 2
    y = (head // 2) * 2 + yl
    other = 1 - yl

    def at(z_, x_, y_, c_):
        return ((z_ * NX + x_) * 2 + y_ % 2, (y_ // 2) * 2 + c_)

    def pair(k):
        p = (pair_index + k + NZ * NX) % (NZ * NX)
        return at(p // NX, p % NX, y, core)

    partner = at(z, x, (head // 2) * 2 + other, core)
    sibling = at(z, x, y, 1 - core)

    def along_y(k):
        return at(z, x, (y + k) % 4, core)

    def along_x(k):
        return at(z, (x + k) % NX, y, core)

    def along_z(k):
        return at((z + k) % NZ, x, y, core)

    peers = [pair(k) for k in (1, -1, 2, -2)]
    peers += [along_y(k) for k in (1, 2, 3)] + [sibling]
    peers += [along_x(k) for k in (1, 2, 3)]
    peers += [along_z(k) for k in range(1, NZ)]
    barrier = pltpu.get_barrier_semaphore()
    for peer in peers:
        pl.semaphore_signal(barrier, inc=1, device_id=peer, device_id_type=MESH)

    w_copy = pltpu.make_async_copy(
        w_ref.at[pl.ds(pl.multiple_of(yl * 192, 8), 192)], wv, w_sem
    )
    w_copy.start()

    pending = []

    def send(src, dst, recv_sem, device):
        copy = pltpu.make_async_remote_copy(
            src_ref=src, dst_ref=dst, send_sem=ss.at[len(pending)], recv_sem=recv_sem,
            device_id=device, device_id_type=MESH,
        )
        copy.start()
        pending.append(copy)

    def arrived(dst, recv_sem):
        pltpu.make_async_remote_copy(
            src_ref=dst, dst_ref=dst, send_sem=ss.at[0], recv_sem=recv_sem,
            device_id=partner, device_id_type=MESH,
        ).wait_recv()

    own = 3 + yl
    theirs = 3 + other

    mine = pl.ds(pl.multiple_of(yl * 192, 8), 192)
    rest = pl.ds(pl.multiple_of(other * 192, 8), 192)
    tkv[0] = k_ref[...].T
    tkv[1] = v_ref[...].T
    tq[...] = (q_ref[...] * SCALE).T
    label = jnp.broadcast_to((seg_ref[...] + 1).astype(F32), (8, B))
    kvs[0:192] = tkv[0, rest]
    kvs[192:384] = tkv[1, rest]
    kvs[384:392] = label
    kvw[own, 0:192] = tkv[0, mine]
    kvw[own, 192:384] = tkv[1, mine]
    kvw[own, 384:392] = label
    qs[...] = tq[rest]
    qw[own] = tq[mine]

    pl.semaphore_wait(barrier, len(peers))

    send(kvs, kvw.at[own], kv_sem.at[own], partner)

    def send_block(window, sem, slot, r):
        send(window.at[slot], window.at[1 + r], sem.at[1 + r], pair(1))
        send(window.at[slot], window.at[5 + r], sem.at[5 + r], pair(-1))
        send(window.at[slot], window.at[7 * (1 - r)], sem.at[7 * (1 - r)], pair(4 * r - 2))

    send_block(kvw, kv_sem, own, yl)
    send(qs, qw.at[own], q_sem.at[own], partner)
    arrived(kvw.at[theirs], kv_sem.at[theirs])
    send_block(kvw, kv_sem, theirs, other)

    cotw[yl, head] = cot_ref[...]
    for k in (1, 2, 3):
        send(cot_ref, cotw.at[yl, head], cot_sem.at[yl * 4 + head], along_y(k))
    send(cot_ref, cotw.at[yl, head], cot_sem.at[yl * 4 + head], sibling)
    for k in (1, 3, 2):
        y_from = (y + k) % 4
        row, col = y_from % 2, (y_from // 2) * 2 + core
        arrived(cotw.at[row, col], cot_sem.at[row * 4 + col])
        send(cotw.at[row, col], cotw.at[row, col], cot_sem.at[row * 4 + col], sibling)
    w_copy.wait()
    hi, mid = split2(wv[...])
    wh[...] = hi
    wm[...] = mid
    for k in range(4):
        y_from = (y + k) % 4
        row, col = y_from % 2, (y_from // 2) * 2 + (1 - core)
        arrived(cotw.at[row, col], cot_sem.at[row * 4 + col])
    for row in range(2):
        for col in range(4):
            tile = cotw[row, col]
            hi, mid = split2(tile)
            coth[row * B:(row + 1) * B, col * 384:(col + 1) * 384] = hi
            cotm[row * B:(row + 1) * B, col * 384:(col + 1) * 384] = mid
            hi, mid = split2(tile.T)
            cotth[col * 384:(col + 1) * 384, row * B:(row + 1) * B] = hi
            cottm[col * 384:(col + 1) * 384, row * B:(row + 1) * B] = mid

    do_t[...] = dot_nt(wh[...], coth[...]) + (
        dot_nt(wh[...], cotm[...]) + dot_nt(wm[...], coth[...])
    )
    dow[3] = do_t[:, :B]
    dow[4] = do_t[:, B:]
    arrived(qw.at[theirs], q_sem.at[theirs])

    for s in range(8):
        if s in (3, 4):
            continue
        arrived(kvw.at[s], kv_sem.at[s])

    send_block(qw, q_sem, own, yl)
    send_block(qw, q_sem, theirs, other)

    def send_two(window, sem, base):
        send(window.at[pl.ds(3, 2)], window.at[pl.ds(1, 2)], sem.at[base], pair(1))
        send(window.at[pl.ds(3, 2)], window.at[pl.ds(5, 2)], sem.at[base + 1], pair(-1))
        send(window.at[4], window.at[0], sem.at[base + 2], pair(2))
        send(window.at[3], window.at[7], sem.at[base + 3], pair(-2))

    def arrived_two(window, sem, base):
        arrived(window.at[pl.ds(1, 2)], sem.at[base])
        arrived(window.at[pl.ds(5, 2)], sem.at[base + 1])
        arrived(window.at[0], sem.at[base + 2])
        arrived(window.at[7], sem.at[base + 3])

    send_two(dow, do_sem, 0)

    for r in range(2):
        lab_col[r * B:(r + 1) * B] = jnp.broadcast_to(kvw[3 + r, 384:385], (B, B)).T
        for h in range(2):
            wide = jnp.full((1, B), band_ref[head * 4 + yl * 2 + h], jnp.int32)
            for s in range(8):
                block = jnp.full((1, B), pair_index * 2 - 3 + s, jnp.int32)
                inside = (wide >= abs(s - 3 - r)) & (block >= 0) & (block < 2 * NZ * NX)
                row = jnp.where(inside, kvw[s, 384:385], -1.0)
                lab_row[r * 2 + h, :, s * B:(s + 1) * B] = jnp.broadcast_to(row, (8, B))

    def window(ref, first):
        return pad_rows(
            jnp.concatenate([ref[s, first:first + HD] for s in range(8)], axis=1)
        )

    def middle(ref, first):
        return pad_rows(
            jnp.concatenate([ref[3, first:first + HD], ref[4, first:first + HD]], axis=1)
        ).T

    lane = lax.broadcasted_iota(jnp.int32, (CHUNK, B), 1)

    def allowed(i, r_block, h):
        column = lab_col[pl.ds(pl.multiple_of(i * CHUNK, CHUNK), CHUNK)]
        row = lab_row[r_block * 2 + h, 0:1]
        return jnp.concatenate([column] * 8, axis=1) == row

    for h in range(2):
        s_ref[...] = mul6(middle(qw, h * HD), window(kvw, h * HD))

        def soften(i, carry, h=h):
            rows = pl.ds(pl.multiple_of(i * CHUNK, CHUNK), CHUNK)
            ok = allowed(i, i // (B // CHUNK), h)
            scores = jnp.where(ok, s_ref[rows], -1e30)
            top = jnp.max(scores, axis=1, keepdims=True)
            e = jnp.exp(scores - top)
            total = jnp.sum(e, axis=1, keepdims=True)
            e_ref[h, rows] = e
            hi, mid = split2(e)
            ph[rows] = hi
            pm[rows] = mid
            log_total = top + jnp.log(total)
            kept = jnp.where(lane == h, log_total, col_ref[rows]) if h else log_total
            col_ref[rows] = jnp.where(lane == 2 + h, 1.0 / total, kept)
            return carry

        lax.fori_loop(0, 2 * B // CHUNK, soften, 0)
        mixed = mul_window(ph[...], pm[...], window(kvw, 192 + h * HD))
        mixed = mixed * col_ref[:, 2 + h:3 + h]
        att_t[h * HD:(h + 1) * HD] = mixed.T[:HD]

    stats = col_ref[...].T
    deltas = [
        jnp.sum(do_t[h * HD:(h + 1) * HD] * att_t[h * HD:(h + 1) * HD], axis=0, keepdims=True)
        for h in range(2)
    ]
    rows = jnp.concatenate(
        [stats[0:2], deltas[0], deltas[1], jnp.zeros((4, 2 * B), F32)], axis=0
    )
    stw[3] = rows[:, :B]
    stw[4] = rows[:, B:]
    send_two(stw, st_sem, 0)

    hi, mid = split2(att_t[...].T)
    ath[...] = hi
    atm[...] = mid
    for col in range(4):
        part = mul3(
            ath[...], atm[...],
            wh[:, col * 384:(col + 1) * 384], wm[:, col * 384:(col + 1) * 384],
        )
        po[col % 2, (col // 2) * 2] = part[:B]
        po[col % 2, (col // 2) * 2 + 1] = part[B:]
    send(po.at[1 - core], por, po_sem, sibling)

    def weigh(i, carry):
        rows = pl.ds(pl.multiple_of(i * 192, 64), 192)
        block = mul3(cotth[rows], cottm[rows], ath[...], atm[...])
        for j in range(NX):
            chunk = block[j * 48:(j + 1) * 48]
            mx[j, i, 0:48] = chunk[:, :B]
            mx[j, i, 48:72] = jnp.concatenate([chunk[:24, B:], chunk[24:, B:]], axis=1)
        return carry

    lax.fori_loop(0, NZ, weigh, 0)
    for k in (1, 2, 3):
        send(mx.at[(x + k) % NX], xr.at[k - 1], x_sem.at[k - 1], along_x(k))

    arrived(por, po_sem)
    for t in range(4):
        ps[t] = po[core, t] + por[t]
    for k in (1, 2, 3):
        send(ps.at[(y + k) % 4], pr.at[k - 1], pr_sem.at[k - 1], along_y(k))

    for h in range(2):
        delta_col = jnp.concatenate([rows[2 + h:3 + h], jnp.zeros((7, 2 * B), F32)], axis=0)
        delta_col = jnp.concatenate([delta_col, jnp.zeros((B - 8, 2 * B), F32)], axis=0).T
        col_ref[...] = jnp.where(
            lax.broadcasted_iota(jnp.int32, (2 * B, B), 1) == 4, delta_col[:, 0:1], col_ref[...]
        )
        gradient = jnp.concatenate([dow[3, h * HD:(h + 1) * HD], dow[4, h * HD:(h + 1) * HD]], axis=1)
        dp_ref[...] = mul4(pad_rows(gradient).T, window(kvw, 192 + h * HD))

        def slope(i, carry, h=h):
            at_rows = pl.ds(pl.multiple_of(i * CHUNK, CHUNK), CHUNK)
            column = col_ref[at_rows]
            probs = e_ref[h, at_rows] * column[:, 2 + h:3 + h]
            hi, mid = split2(probs * (dp_ref[at_rows] - column[:, 4:5]))
            ph[at_rows] = hi
            pm[at_rows] = mid
            return carry

        lax.fori_loop(0, 2 * B // CHUNK, slope, 0)
        result = (mul_window(ph[...], pm[...], window(kvw, h * HD)) * SCALE).T[:HD]
        gown[0, h * HD:(h + 1) * HD] = jnp.where(yl == 0, result[:, :B], result[:, B:])
        gsend[0, h * HD:(h + 1) * HD] = jnp.where(yl == 0, result[:, B:], result[:, :B])
    send(gsend.at[0], grecv.at[0], g_sem.at[0], partner)

    for k in (1, 2, 3):
        arrived(xr.at[k - 1], x_sem.at[k - 1])
    xs[...] = mx[x] + xr[0] + xr[1] + xr[2]
    for k in range(1, NZ):
        send(xs.at[(z + k) % NZ], zr.at[k - 1], z_sem.at[k - 1], along_z(k))

    for s in range(8):
        if s in (3, 4):
            continue
        arrived(qw.at[s], q_sem.at[s])
    arrived_two(dow, do_sem, 0)
    arrived_two(stw, st_sem, 0)
    for h in range(2):
        s_ref[...] = mul6(middle(kvw, h * HD), window(qw, h * HD))
        dp_ref[...] = mul4(middle(kvw, 192 + h * HD), window(dow, h * HD))
        log_row = jnp.concatenate([stw[s, h:h + 1] for s in range(8)], axis=1)
        delta_row = jnp.concatenate([stw[s, 2 + h:3 + h] for s in range(8)], axis=1)

        def weigh_keys(i, carry, h=h, log_row=log_row, delta_row=delta_row):
            at_rows = pl.ds(pl.multiple_of(i * CHUNK, CHUNK), CHUNK)
            ok = allowed(i, i // (B // CHUNK), h)
            probs = jnp.exp(jnp.where(ok, s_ref[at_rows] - log_row, -1e30))
            hi, mid = split2(probs)
            ph[at_rows] = hi
            pm[at_rows] = mid
            dp_ref[at_rows] = probs * (dp_ref[at_rows] - delta_row)
            return carry

        lax.fori_loop(0, 2 * B // CHUNK, weigh_keys, 0)
        value_part = mul_window(ph[...], pm[...], window(dow, h * HD)).T[:HD]
        hi, mid = split2(dp_ref[...])
        key_part = mul_window(hi, mid, window(qw, h * HD)).T[:HD]
        for n, result in ((1, key_part), (2, value_part)):
            gown[n, h * HD:(h + 1) * HD] = jnp.where(yl == 0, result[:, :B], result[:, B:])
            gsend[n, h * HD:(h + 1) * HD] = jnp.where(yl == 0, result[:, B:], result[:, :B])
    send(gsend.at[1], grecv.at[1], g_sem.at[1], partner)
    send(gsend.at[2], grecv.at[2], g_sem.at[2], partner)

    for k in (1, 2, 3):
        arrived(pr.at[k - 1], pr_sem.at[k - 1])
    out_ref[...] = ps[y] + pr[0] + pr[1] + pr[2]

    total = xs[z]
    for k in range(1, NZ):
        arrived(zr.at[k - 1], z_sem.at[k - 1])
        total = total + zr[k - 1]
    gsum[...] = total
    send(gsum, yr, y_sem, partner)

    for n, ref in enumerate((gq_ref, gk_ref, gv_ref)):
        arrived(grecv.at[n], g_sem.at[n])
        lower = jnp.where(yl == 0, gown[n], grecv[n])
        upper = jnp.where(yl == 0, grecv[n], gown[n])
        ref[...] = jnp.concatenate([lower, upper], axis=0).T

    arrived(yr, y_sem)
    lower = jnp.where(yl == 0, gsum[...], yr[...])
    upper = jnp.where(yl == 0, yr[...], gsum[...])
    pieces = []
    for part in (lower, upper):
        pieces.append(jnp.where(yl == 0, part[0:24], part[24:48]).T)
        last = part[48:72].T
        pieces.append(jnp.where(yl == 0, last[:64], last[64:]))
    gw_ref[...] = jnp.concatenate(pieces, axis=0)

    for copy in pending:
        copy.wait_send()


SENDS = 66


def shards(query, key, value, segment, band, out_weight, cotangent):
    vmem = pl.BlockSpec(memory_space=pltpu.VMEM)

    def full(*shape):
        return pltpu.VMEM(shape, F32)

    def half(*shape):
        return pltpu.VMEM(shape, BF16)

    block = jax.ShapeDtypeStruct((B, 384), F32)
    dma = pltpu.SemaphoreType.DMA
    return pl.pallas_call(
        kernel,
        out_shape=(block, block, block, block, jax.ShapeDtypeStruct((384, 24), F32)),
        in_specs=[
            vmem, vmem, vmem, vmem,
            pl.BlockSpec(memory_space=pltpu.SMEM),
            pl.BlockSpec(memory_space=pl.ANY),
            vmem,
        ],
        out_specs=[vmem] * 5,
        scratch_shapes=[
            full(384, B), full(2, 384, B), full(392, B), full(8, 392, B),
            full(192, B), full(8, 192, B), full(8, 192, B), full(8, 8, B),
            full(2, 4, B, 384), full(192, 1536), full(2 * B, B), full(4, 8, W8),
            half(2 * B, 1536), half(2 * B, 1536), half(1536, 2 * B), half(1536, 2 * B),
            half(192, 1536), half(192, 1536),
            full(2 * B, W8), full(2, 2 * B, W8), full(2 * B, W8),
            half(2 * B, W8), half(2 * B, W8), full(2 * B, B),
            full(192, 2 * B), full(192, 2 * B), half(2 * B, 192), half(2 * B, 192),
            full(2, 4, B, 384), full(4, B, 384), full(4, B, 384), full(3, B, 384),
            full(NX, NZ, 72, B), full(3, NZ, 72, B), full(NZ, 72, B), full(NZ - 1, 72, B),
            full(72, B), full(72, B), full(3, 192, B), full(3, 192, B), full(3, 192, B),
            dma((SENDS,)), dma((8,)), dma((8,)), dma((4,)), dma((4,)), dma((8,)), dma,
            dma, dma((3,)), dma((3,)), dma((NZ - 1,)), dma((3,)), dma,
        ],
        compiler_params=pltpu.CompilerParams(
            collective_id=0, has_side_effects=True, vmem_limit_bytes=58 * 2**20
        ),
        name="banded_attention",
    )(query, key, value, segment.reshape(1, B), band, out_weight, cotangent)


def solution(mesh):
    in_specs = (
        P("ctx", "head"),
        P("ctx", "head"),
        P("ctx", "head"),
        P("ctx"),
        P(),
        P("head", None),
        P("ctx", "head"),
    )
    out_specs = (
        P("ctx", "head"),
        P("ctx", "head"),
        P("ctx", "head"),
        P("ctx", "head"),
        P("head", "ctx"),
    )
    return jax.shard_map(shards, mesh=mesh, in_specs=in_specs, out_specs=out_specs, check_vma=False)
```

time: 546 us -> 90.1 us (0.17); the launches traced: 539 us -> 89.8 us
  waiting for transfers between devices: 258 us -> 0 us
  starting transfers between devices: 110 us -> 0 us
  Pallas kernels: 0 us -> 81.1 us
  matrix products: 75 us -> 0 us
  local copies, waits for them, and re-layouts: 54 us -> 8.11 us
  other arithmetic: 16.7 us -> 0 us
  between operations: 15.4 us -> 0.64 us
  blocking collectives: 9.91 us -> 0 us
    unnamed x3 -> x0, waiting for transfers between devices: 255 us -> none
    ppermute x30 -> x0, starting transfers between devices: 110 us -> none  [passed_along(): return lax.ppermute(block, axis, route)]
    pallas_call x0 -> x1, Pallas kernels: none -> 81.1 us  [shards(): pl.pallas_call(kernel, out_shape=(block, block, block, block, jax.ShapeDt...]
    dot_general x45 -> x0, matrix products: 75 us -> none  [the longest x7 18.6 us: tile_scores(): jnp.einsum('ihe,jhe->hij', query_heads, shaped(keys_tile), precision=high...]
    reshape x14 -> x0, local copies, waits for them, and re-layouts: 23.5 us -> none  [the longest x7 12.3 us: shards(): key_part.reshape(frame_rows, local_width)]
    ppermute x12 -> x0, local copies, waits for them, and re-layouts: 20.8 us -> none  [passed_along(): return lax.ppermute(block, axis, route)]
    all_gather x1 -> x0, blocking collectives: 9.91 us -> none  [shards(): piece = lax.all_gather(cotangent, 'head', axis=1, tiled=True)]
    add x12 -> x0, other arithmetic: 7.96 us -> none  [the longest x2 1.75 us: shards(): toward_below[1] + parts[-distance][1]]
  transfers between devices with their start and end apart: 32 -> 0, of which waited for: 2 -> 0; matrix products, arithmetic and copies ran while one was open for 24% -> 0% of each run, Pallas kernels for 0% -> 0%
where the time goes in v1:
time: 90.1 us; the launch traced here: 89.8 us
  Pallas kernels  81.1 us (90%)
  local copies, waits for them, and re-layouts  8.11 us (9%)
    pallas_call x1, Pallas kernels, shards(): pl.pallas_call(kernel, out_shape=(block, block, block, block, jax.ShapeDt...  81.1 us
    unnamed x4, local copies, waits for them, and re-layouts  6.46 us

profile of v1, /device:TPU:8, one launch (start us, length us, event | category | flops | bytes accessed | tf_op | source)
XLA Modules:
  0.0 89.8 jit_solution(12820933139186162706)
XLA Ops:
  0.6 81.1 %banded_attention.1 = (f32[128,384]{1,0:T(8,128)}, f32[128,384]{1,0:T(8,128)}, f32[128,384]{1,0:T(8,128)}, f32[128,384]{1,0:T(8,128)}, f32[384,24]{1,0:T(8,128)}) custom-call(f32[128,384]{1,0:T(8,128)} %q_ref.1, f32[128,384]{1,0:T(8,128)} %k_ref.1, f32[128,384]{1,0:T(8,128)} %v_ref.1, s32[1,128]{1,0:T(1,128)} %bitcast.1, s32[16]{0:T(128)} %band_ref.1, ...), custom_call_target="tpu_custom_call" | custom-call | tf_op jit(solution)/shard_map/banded_attention/pallas_call | solution.py:429
  81.7 1.6 %copy.12 = f32[384,24]{0,1:T(8,128)} copy(f32[384,24]{1,0:T(8,128)} %get-tuple-element.9) | data formatting | bytes 73728 | tf_op jit(solution)/shard_map/banded_attention/pallas_call | solution.py:429
  83.4 1.6 %copy.17 = f32[128,384]{1,0:T(8,128)} copy(f32[128,384]{1,0:T(8,128)} %get-tuple-element.15) | data formatting | bytes 393216
  85.0 1.6 %copy.18 = f32[128,384]{1,0:T(8,128)} copy(f32[128,384]{1,0:T(8,128)} %get-tuple-element.16) | data formatting | bytes 393216
  86.6 1.6 %copy.19 = f32[128,384]{1,0:T(8,128)} copy(f32[128,384]{1,0:T(8,128)} %get-tuple-element.17) | data formatting | bytes 393216
  88.2 1.6 %copy.20 = f32[128,384]{1,0:T(8,128)} copy(f32[128,384]{1,0:T(8,128)} %get-tuple-element.18) | data formatting | bytes 393216

commit v2 on v1

v2 whole, which is shorter than its diff:
```python
import math

import jax
import jax.numpy as jnp
from jax import lax
from jax.experimental import pallas as pl
from jax.experimental.pallas import tpu as pltpu
from jax.sharding import PartitionSpec as P

MESH = pl.DeviceIdType.MESH
F32 = jnp.float32
BF16 = jnp.bfloat16
HD = 96
SCALE = 1.0 / math.sqrt(HD)
B = 128
W8 = 8 * B
NZ, NX = 8, 4
CHUNK = 32


def split2(x):
    hi = x.astype(BF16)
    return hi, (x - hi.astype(F32)).astype(BF16)


def split3(x):
    hi = x.astype(BF16)
    rest = x - hi.astype(F32)
    mid = rest.astype(BF16)
    return hi, mid, (rest - mid.astype(F32)).astype(BF16)


def dot(a, b):
    return jnp.dot(a, b, preferred_element_type=F32)


def dot_nt(a, b):
    return lax.dot_general(a, b, (((1,), (1,)), ((), ())), preferred_element_type=F32)


def pad_rows(x):
    return jnp.concatenate([x, jnp.zeros((B - HD, x.shape[1]), x.dtype)], axis=0)


def mul6(left, right):
    lh, lm, ll = split3(left)
    rh, rm, rl = split3(right)
    return dot(
        jnp.concatenate([lh, lh, lm, lm, lh, ll], axis=1),
        jnp.concatenate([rh, rm, rh, rm, rl, rh], axis=0),
    )


def mul_window(hi, mid, right):
    rh, rm = split2(right)
    both = jnp.concatenate([rh, rm], axis=0)
    out = dot_nt(hi, both) + dot_nt(mid, both)
    return out[:, :B] + out[:, B:]


def mul_parts(lh, lm, rh, rm):
    return (dot(lh, rh) + dot(lm, rm)) + (dot(lh, rm) + dot(lm, rh))


def kernel(
    q_ref, k_ref, v_ref, seg_ref, band_ref, w_ref, cot_ref,
    out_ref, gq_ref, gk_ref, gv_ref, gw_ref,
    tq, tkv, ks, vs, kw, vw, qs, qw, dow, stw, cotw, wv, lab_col, lab_row,
    coth, cotm, cotl, cotth, cottm, wh, wm, wl,
    s_ref, e_ref, dp_ref, ph, pm, col_ref, att_t, do_t, ath, atm,
    po, por, ps, pf, pr, mx, xfu, xfd, xr, xs, zr, gsum, yr, gown, gsend, grecv,
    ss, k_sem, v_sem, q_sem, do_sem, st_sem, cot_sem, y_sem, po_sem, pr_sem, x_sem, z_sem, g_sem, w_sem,
):
    ctx = lax.axis_index("ctx")
    head = lax.axis_index("head")
    yl = ctx % 2
    pair_index = ctx // 2
    z, x = pair_index // NX, pair_index % NX
    core = head % 2
    y = (head // 2) * 2 + yl
    other = 1 - yl

    def at(z_, x_, y_, c_):
        return ((z_ * NX + x_) * 2 + y_ % 2, (y_ // 2) * 2 + c_)

    def pair(k):
        p = (pair_index + k + NZ * NX) % (NZ * NX)
        return at(p // NX, p % NX, y, core)

    partner = at(z, x, (head // 2) * 2 + other, core)
    sibling = at(z, x, y, 1 - core)

    def along_y(k):
        return at(z, x, (y + k) % 4, core)

    def along_x(k):
        return at(z, (x + k) % NX, y, core)

    def along_z(k):
        return at((z + k) % NZ, x, y, core)

    peers = [pair(k) for k in (1, -1, 2, -2)]
    peers += [along_y(k) for k in (1, 2, 3)] + [sibling]
    peers += [along_x(k) for k in (1, 2, 3)]
    peers += [along_z(k) for k in range(1, NZ)]
    barrier = pltpu.get_barrier_semaphore()
    for peer in peers:
        pl.semaphore_signal(barrier, inc=1, device_id=peer, device_id_type=MESH)

    w_copy = pltpu.make_async_copy(
        w_ref.at[pl.ds(pl.multiple_of(yl * 192, 8), 192)], wv, w_sem
    )
    w_copy.start()

    pending = []

    def send(src, dst, recv_sem, device):
        copy = pltpu.make_async_remote_copy(
            src_ref=src, dst_ref=dst, send_sem=ss.at[len(pending)], recv_sem=recv_sem,
            device_id=device, device_id_type=MESH,
        )
        copy.start()
        pending.append(copy)

    def arrived(dst, recv_sem):
        pltpu.make_async_remote_copy(
            src_ref=dst, dst_ref=dst, send_sem=ss.at[0], recv_sem=recv_sem,
            device_id=partner, device_id_type=MESH,
        ).wait_recv()

    own = 3 + yl
    theirs = 3 + other

    mine = pl.ds(pl.multiple_of(yl * 192, 8), 192)
    rest = pl.ds(pl.multiple_of(other * 192, 8), 192)
    tkv[0] = k_ref[...].T
    label = jnp.broadcast_to((seg_ref[...] + 1).astype(F32), (8, B))
    ks[0:192] = tkv[0, rest]
    ks[192:200] = label
    kw[own, 0:192] = tkv[0, mine]
    kw[own, 192:200] = label
    tkv[1] = v_ref[...].T
    vs[...] = tkv[1, rest]
    vw[own] = tkv[1, mine]
    tq[...] = (q_ref[...] * SCALE).T
    qs[...] = tq[rest]
    qw[own] = tq[mine]

    pl.semaphore_wait(barrier, len(peers))

    def send_block(window, sem, slot, r):
        send(window.at[slot], window.at[1 + r], sem.at[1 + r], pair(1))
        send(window.at[slot], window.at[5 + r], sem.at[5 + r], pair(-1))

    def relay(window, sem):
        arrived(window.at[2], sem.at[2])
        send(window.at[2], window.at[0], sem.at[0], pair(1))
        arrived(window.at[5], sem.at[5])
        send(window.at[5], window.at[7], sem.at[7], pair(-1))

    def arrived_window(window, sem):
        for slot in (1, 6, 0, 7):
            arrived(window.at[slot], sem.at[slot])

    send(ks, kw.at[own], k_sem.at[own], partner)
    send(vs, vw.at[own], v_sem.at[own], partner)
    send_block(kw, k_sem, own, yl)
    send_block(vw, v_sem, own, yl)
    send(qs, qw.at[own], q_sem.at[own], partner)
    cotw[yl, head] = cot_ref[...]
    arrived(kw.at[theirs], k_sem.at[theirs])
    send_block(kw, k_sem, theirs, other)
    arrived(vw.at[theirs], v_sem.at[theirs])
    send_block(vw, v_sem, theirs, other)

    def cot_slot(k, c):
        y_from = (y + k) % 4
        return y_from % 2, (y_from // 2) * 2 + c

    def cot_get(k, c, *part):
        row, col = cot_slot(k, c)
        sem = cot_sem.at[row * 4 + col, part[0].start // 64 if part else 0]
        arrived(cotw.at[(row, col, *part)], sem)

    def cot_send(k, device, *part):
        row, col = cot_slot(k, core)
        piece = cotw.at[(row, col, *part)]
        send(piece, piece, cot_sem.at[row * 4 + col, part[0].start // 64 if part else 0], device)

    halves = pl.ds(0, 64), pl.ds(64, 64)
    cot_send(0, along_y(1))
    cot_send(0, along_y(3))
    cot_send(0, sibling)
    relay(kw, k_sem)
    w_copy.wait()
    hi, mid, low = split3(wv[...])
    wh[...] = hi
    wm[...] = mid
    wl[...] = low
    cot_get(3, core)
    cot_send(3, along_y(1), halves[0])
    cot_get(1, core)
    cot_send(1, along_y(3), halves[1])
    cot_send(3, sibling)
    cot_send(1, sibling)
    relay(vw, v_sem)
    arrived(qw.at[theirs], q_sem.at[theirs])
    send_block(qw, q_sem, own, yl)
    send_block(qw, q_sem, theirs, other)
    arrived_window(kw, k_sem)

    for r in range(2):
        lab_col[r * B:(r + 1) * B] = jnp.broadcast_to(kw[3 + r, 192:193], (B, B)).T
        for h in range(2):
            wide = jnp.full((1, B), band_ref[head * 4 + yl * 2 + h], jnp.int32)
            for s in range(8):
                block = jnp.full((1, B), pair_index * 2 - 3 + s, jnp.int32)
                inside = (wide >= abs(s - 3 - r)) & (block >= 0) & (block < 2 * NZ * NX)
                row = jnp.where(inside, kw[s, 192:193], -1.0)
                lab_row[r * 2 + h, :, s * B:(s + 1) * B] = jnp.broadcast_to(row, (8, B))

    def window(ref, first):
        return pad_rows(
            jnp.concatenate([ref[s, first:first + HD] for s in range(8)], axis=1)
        )

    def middle(ref, first):
        return pad_rows(
            jnp.concatenate([ref[3, first:first + HD], ref[4, first:first + HD]], axis=1)
        ).T

    lane = lax.broadcasted_iota(jnp.int32, (CHUNK, B), 1)

    def allowed(i, r_block, h):
        column = lab_col[pl.ds(pl.multiple_of(i * CHUNK, CHUNK), CHUNK)]
        row = lab_row[r_block * 2 + h, 0:1]
        return jnp.concatenate([column] * 8, axis=1) == row

    for h in range(2):
        s_ref[...] = mul6(middle(qw, h * HD), window(kw, h * HD))

        def soften(i, carry, h=h):
            rows = pl.ds(pl.multiple_of(i * CHUNK, CHUNK), CHUNK)
            ok = allowed(i, i // (B // CHUNK), h)
            scores = jnp.where(ok, s_ref[rows], -1e30)
            top = jnp.max(scores, axis=1, keepdims=True)
            e = jnp.exp(scores - top)
            total = jnp.sum(e, axis=1, keepdims=True)
            e_ref[h, rows] = e
            hi, mid = split2(e)
            ph[h, rows] = hi
            pm[h, rows] = mid
            log_total = top + jnp.log(total)
            kept = jnp.where(lane == h, log_total, col_ref[rows]) if h else log_total
            col_ref[rows] = jnp.where(lane == 2 + h, 1.0 / total, kept)
            return carry

        lax.fori_loop(0, 2 * B // CHUNK, soften, 0, unroll=True)

    for part in halves:
        cot_get(2, core, part)
        cot_send(2, sibling, part)
    for k in (0, 1, 3):
        cot_get(k, 1 - core)
    for part in halves:
        cot_get(2, 1 - core, part)
    for row in range(2):
        for col in range(4):
            tile = cotw[row, col]
            hi, mid, low = split3(tile)
            coth[row * B:(row + 1) * B, col * 384:(col + 1) * 384] = hi
            cotm[row * B:(row + 1) * B, col * 384:(col + 1) * 384] = mid
            cotl[row * B:(row + 1) * B, col * 384:(col + 1) * 384] = low
            hi, mid = split2(tile.T)
            cotth[col * 384:(col + 1) * 384, row * B:(row + 1) * B] = hi
            cottm[col * 384:(col + 1) * 384, row * B:(row + 1) * B] = mid

    arrived_window(vw, v_sem)

    for h in range(2):
        mixed = mul_window(ph[h], pm[h], window(vw, h * HD))
        mixed = mixed * col_ref[:, 2 + h:3 + h]
        att_t[h * HD:(h + 1) * HD] = mixed.T[:HD]

    hi, mid = split2(att_t[...].T)
    ath[...] = hi
    atm[...] = mid
    def weigh(i, carry):
        rows = pl.ds(pl.multiple_of(i * 192, 64), 192)
        slot = (i - z + 2 * NZ - 2) % NZ
        block = mul_parts(cotth[rows], cottm[rows], ath[...], atm[...])
        for j in range(NX):
            chunk = block[j * 48:(j + 1) * 48]
            mx[j, slot, 0:48] = chunk[:, :B]
            mx[j, slot, 48:72] = jnp.concatenate([chunk[:24, B:], chunk[24:, B:]], axis=1)
        return carry

    lax.fori_loop(0, NZ, weigh, 0)
    far = (x + 2) % NX
    up, down = (x + 1) % NX, (x + 3) % NX
    thirds = pl.ds(0, 40), pl.ds(40, 32)
    quads = pl.ds(0, 4), pl.ds(4, 4)
    for n, quad in enumerate(quads):
        send(mx.at[far, quad, thirds[0]], xfu.at[n], x_sem.at[n], along_x(1))
        send(mx.at[far, quad, thirds[1]], xfd.at[n], x_sem.at[2 + n], along_x(3))

    relay(qw, q_sem)
    do_t[...] = (dot_nt(wh[...], coth[...]) + dot_nt(wm[...], cotm[...])) + (
        (dot_nt(wh[...], cotm[...]) + dot_nt(wm[...], coth[...]))
        + (dot_nt(wh[...], cotl[...]) + dot_nt(wl[...], coth[...]))
    )
    dow[3] = do_t[:, :B]
    dow[4] = do_t[:, B:]

    def send_two(window, sem, base):
        send(window.at[pl.ds(3, 2)], window.at[pl.ds(1, 2)], sem.at[base], pair(1))
        send(window.at[pl.ds(3, 2)], window.at[pl.ds(5, 2)], sem.at[base + 1], pair(-1))

    def relay_two(window, sem, base):
        arrived(window.at[pl.ds(1, 2)], sem.at[base])
        send(window.at[2], window.at[0], sem.at[base + 2], pair(1))
        arrived(window.at[pl.ds(5, 2)], sem.at[base + 1])
        send(window.at[5], window.at[7], sem.at[base + 3], pair(-1))

    def arrived_two(window, sem, base):
        arrived(window.at[0], sem.at[base + 2])
        arrived(window.at[7], sem.at[base + 3])

    send_two(dow, do_sem, 0)
    stats = col_ref[...].T
    deltas = [
        jnp.sum(do_t[h * HD:(h + 1) * HD] * att_t[h * HD:(h + 1) * HD], axis=0, keepdims=True)
        for h in range(2)
    ]
    rows = jnp.concatenate(
        [stats[0:2], deltas[0], deltas[1], jnp.zeros((4, 2 * B), F32)], axis=0
    )
    stw[3] = rows[:, :B]
    stw[4] = rows[:, B:]
    send_two(stw, st_sem, 0)
    send(stw.at[4], stw.at[0], st_sem.at[2], pair(2))
    send(stw.at[3], stw.at[7], st_sem.at[3], pair(-2))
    for n, quad in enumerate(quads):
        arrived(xfu.at[n], x_sem.at[n])
        mx[up, quad, thirds[0]] = mx[up, quad, thirds[0]] + xfu[n]
        send(mx.at[up, quad], xr.at[0, n], x_sem.at[4 + n], along_x(1))
        arrived(xfd.at[n], x_sem.at[2 + n])
        mx[down, quad, thirds[1]] = mx[down, quad, thirds[1]] + xfd[n]
        send(mx.at[down, quad], xr.at[1, n], x_sem.at[6 + n], along_x(3))
    relay_two(dow, do_sem, 0)

    for col in range(4):
        part = mul_parts(
            ath[...], atm[...],
            wh[:, col * 384:(col + 1) * 384], wm[:, col * 384:(col + 1) * 384],
        )
        po[col % 2, (col // 2) * 2] = part[:B]
        po[col % 2, (col // 2) * 2 + 1] = part[B:]
    send(po.at[1 - core], por, po_sem, sibling)

    arrived(por, po_sem)
    for t in range(4):
        ps[t] = po[core, t] + por[t]
    far_y, up_y, down_y = (y + 2) % 4, (y + 1) % 4, (y + 3) % 4
    send(ps.at[far_y, halves[0]], pf.at[0], pr_sem.at[0], along_y(1))
    send(ps.at[far_y, halves[1]], pf.at[1], pr_sem.at[1], along_y(3))

    def give(n, h, result):
        gown[n, h] = jnp.where(yl == 0, result[:, :B], result[:, B:])
        gsend[n, h] = jnp.where(yl == 0, result[:, B:], result[:, :B])
        send(gsend.at[n, h], grecv.at[n, h], g_sem.at[n * 2 + h], partner)

    for h in range(2):
        delta_col = jnp.concatenate([rows[2 + h:3 + h], jnp.zeros((7, 2 * B), F32)], axis=0)
        delta_col = jnp.concatenate([delta_col, jnp.zeros((B - 8, 2 * B), F32)], axis=0).T
        col_ref[...] = jnp.where(
            lax.broadcasted_iota(jnp.int32, (2 * B, B), 1) == 4, delta_col[:, 0:1], col_ref[...]
        )
        gradient = jnp.concatenate([dow[3, h * HD:(h + 1) * HD], dow[4, h * HD:(h + 1) * HD]], axis=1)
        dp_ref[...] = mul6(pad_rows(gradient).T, window(vw, h * HD))

        def slope(i, carry, h=h):
            at_rows = pl.ds(pl.multiple_of(i * CHUNK, CHUNK), CHUNK)
            column = col_ref[at_rows]
            probs = e_ref[h, at_rows] * column[:, 2 + h:3 + h]
            hi, mid = split2(probs * (dp_ref[at_rows] - column[:, 4:5]))
            ph[h, at_rows] = hi
            pm[h, at_rows] = mid
            return carry

        lax.fori_loop(0, 2 * B // CHUNK, slope, 0, unroll=True)
        result = (mul_window(ph[h], pm[h], window(kw, h * HD)) * SCALE).T[:HD]
        give(0, h, result)
        if h == 0:
            arrived(pf.at[0], pr_sem.at[0])
            ps[up_y, 0:64] = ps[up_y, 0:64] + pf[0]
            send(ps.at[up_y], pr.at[0], pr_sem.at[2], along_y(1))
            arrived(pf.at[1], pr_sem.at[1])
            ps[down_y, 64:128] = ps[down_y, 64:128] + pf[1]
            send(ps.at[down_y], pr.at[1], pr_sem.at[3], along_y(3))

    def sum_half(n):
        arrived(xr.at[0, n], x_sem.at[4 + n])
        arrived(xr.at[1, n], x_sem.at[6 + n])
        xs[quads[n]] = mx[x, quads[n]] + xr[0, n] + xr[1, n]
        for k in ((4, 3, 5, 2), (6, 7, 1))[n]:
            send(xs.at[(k + 6) % NZ], zr.at[k - 1], z_sem.at[k - 1], along_z(k))

    sum_half(0)

    arrived_window(qw, q_sem)
    arrived(stw.at[pl.ds(1, 2)], st_sem.at[0])
    arrived(stw.at[pl.ds(5, 2)], st_sem.at[1])
    arrived_two(stw, st_sem, 0)
    arrived_two(dow, do_sem, 0)
    for h in range(2):
        s_ref[...] = mul6(middle(kw, h * HD), window(qw, h * HD))
        dp_ref[...] = mul6(middle(vw, h * HD), window(dow, h * HD))
        log_row = jnp.concatenate([stw[s, h:h + 1] for s in range(8)], axis=1)
        delta_row = jnp.concatenate([stw[s, 2 + h:3 + h] for s in range(8)], axis=1)

        def weigh_keys(i, carry, h=h, log_row=log_row, delta_row=delta_row):
            at_rows = pl.ds(pl.multiple_of(i * CHUNK, CHUNK), CHUNK)
            ok = allowed(i, i // (B // CHUNK), h)
            probs = jnp.exp(jnp.where(ok, s_ref[at_rows] - log_row, -1e30))
            hi, mid = split2(probs)
            ph[h, at_rows] = hi
            pm[h, at_rows] = mid
            dp_ref[at_rows] = probs * (dp_ref[at_rows] - delta_row)
            return carry

        lax.fori_loop(0, 2 * B // CHUNK, weigh_keys, 0, unroll=True)
        give(2, h, mul_window(ph[h], pm[h], window(dow, h * HD)).T[:HD])
        hi, mid = split2(dp_ref[...])
        give(1, h, mul_window(hi, mid, window(qw, h * HD)).T[:HD])
        if h == 0:
            sum_half(1)

    arrived(pr.at[0], pr_sem.at[2])
    arrived(pr.at[1], pr_sem.at[3])
    out_ref[...] = ps[y] + pr[0] + pr[1]

    total = xs[6]
    for k in range(1, NZ):
        arrived(zr.at[k - 1], z_sem.at[k - 1])
        total = total + zr[k - 1]
    gsum[...] = total
    send(gsum, yr, y_sem, partner)

    for n, ref in enumerate((gq_ref, gk_ref, gv_ref)):
        for h in range(2):
            arrived(grecv.at[n, h], g_sem.at[n * 2 + h])
        lower = [jnp.where(yl == 0, gown[n, h], grecv[n, h]) for h in range(2)]
        upper = [jnp.where(yl == 0, grecv[n, h], gown[n, h]) for h in range(2)]
        ref[...] = jnp.concatenate(lower + upper, axis=0).T

    arrived(yr, y_sem)
    lower = jnp.where(yl == 0, gsum[...], yr[...])
    upper = jnp.where(yl == 0, yr[...], gsum[...])
    pieces = []
    for part in (lower, upper):
        pieces.append(jnp.where(yl == 0, part[0:24], part[24:48]))
        last = part[48:72]
        pieces.append(jnp.where(yl == 0, last[:, :64], last[:, 64:]))
    gw_ref[...] = jnp.concatenate(pieces, axis=1)

    assert len(pending) == SENDS
    for copy in pending:
        copy.wait_send()


SENDS = 65


def hand_over(*refs):
    for n in range(5):
        refs[5 + n][...] = refs[n][...]


def shards(query, key, value, segment, band, out_weight, cotangent):
    vmem = pl.BlockSpec(memory_space=pltpu.VMEM)

    def full(*shape):
        return pltpu.VMEM(shape, F32)

    def half(*shape):
        return pltpu.VMEM(shape, BF16)

    block = jax.ShapeDtypeStruct((B, 384), F32)
    dma = pltpu.SemaphoreType.DMA
    results = pl.pallas_call(
        kernel,
        out_shape=(block, block, block, block, jax.ShapeDtypeStruct((24, 384), F32)),
        in_specs=[
            vmem, vmem, vmem, vmem,
            pl.BlockSpec(memory_space=pltpu.SMEM),
            pl.BlockSpec(memory_space=pl.ANY),
            vmem,
        ],
        out_specs=[vmem] * 5,
        scratch_shapes=[
            full(384, B), full(2, 384, B), full(200, B), full(192, B), full(8, 200, B), full(8, 192, B),
            full(192, B), full(8, 192, B), full(8, 192, B), full(8, 8, B),
            full(2, 4, B, 384), full(192, 1536), full(2 * B, B), full(4, 8, W8),
            half(2 * B, 1536), half(2 * B, 1536), half(2 * B, 1536), half(1536, 2 * B), half(1536, 2 * B),
            half(192, 1536), half(192, 1536), half(192, 1536),
            full(2 * B, W8), full(2, 2 * B, W8), full(2 * B, W8),
            half(2, 2 * B, W8), half(2, 2 * B, W8), full(2 * B, B),
            full(192, 2 * B), full(192, 2 * B), half(2 * B, 192), half(2 * B, 192),
            full(2, 4, B, 384), full(4, B, 384), full(4, B, 384), full(2, 64, 384), full(2, B, 384),
            full(NX, NZ, 72, B), full(2, 4, 40, B), full(2, 4, 32, B), full(2, 2, 4, 72, B), full(NZ, 72, B), full(NZ - 1, 72, B),
            full(72, B), full(72, B), full(3, 2, HD, B), full(3, 2, HD, B), full(3, 2, HD, B),
            dma((SENDS,)), dma((8,)), dma((8,)), dma((8,)), dma((4,)), dma((4,)), dma((8, 2)), dma,
            dma, dma((4,)), dma((8,)), dma((NZ - 1,)), dma((6,)), dma,
        ],
        compiler_params=pltpu.CompilerParams(
            collective_id=0, has_side_effects=True, vmem_limit_bytes=58 * 2**20
        ),
        name="banded_attention",
    )(query, key, value, segment.reshape(1, B), band, out_weight, cotangent)
    *blocks, weight = pl.pallas_call(
        hand_over,
        out_shape=[jax.ShapeDtypeStruct(r.shape, F32) for r in results],
        in_specs=[vmem] * 5,
        out_specs=[vmem] * 5,
        compiler_params=pltpu.CompilerParams(vmem_limit_bytes=58 * 2**20),
        name="hand_over",
    )(*results)
    return (*blocks, weight.T)


def solution(mesh):
    in_specs = (
        P("ctx", "head"),
        P("ctx", "head"),
        P("ctx", "head"),
        P("ctx"),
        P(),
        P("head", None),
        P("ctx", "head"),
    )
    out_specs = (
        P("ctx", "head"),
        P("ctx", "head"),
        P("ctx", "head"),
        P("ctx", "head"),
        P("head", "ctx"),
    )
    return jax.shard_map(shards, mesh=mesh, in_specs=in_specs, out_specs=out_specs, check_vma=False)
```

time: 90.1 us -> 72.4 us (0.80)
  Pallas kernels: 81.1 us -> 71.6 us
  local copies, waits for them, and re-layouts: 8.11 us -> 0 us
    pallas_call x1, Pallas kernels: 81.1 us -> 69.5 us  [shards(): pl.pallas_call(kernel, out_shape=(block, block, block, block, jax.ShapeDt...]
    unnamed x4 -> x0, local copies, waits for them, and re-layouts: 6.46 us -> none
    pallas_call x0 -> x1, Pallas kernels: none -> 2.11 us  [shards(): pl.pallas_call(hand_over, out_shape=[jax.ShapeDtypeStruct(r.shape, F32) f...]
    pallas_call x1 -> x0, local copies, waits for them, and re-layouts: 1.65 us -> none  [shards(): pl.pallas_call(kernel, out_shape=(block, block, block, block, jax.ShapeDt...]
where the time goes in v2:
time: 72.4 us; the launch traced here: 72.2 us
  Pallas kernels  71.6 us (99%)
    pallas_call x1, Pallas kernels, shards(): pl.pallas_call(kernel, out_shape=(block, block, block, block, jax.ShapeDt...  69.5 us
    pallas_call x1, Pallas kernels, shards(): pl.pallas_call(hand_over, out_shape=[jax.ShapeDtypeStruct(r.shape, F32) f...  2.11 us

profile of v2, /device:TPU:8, one launch (start us, length us, event | category | flops | bytes accessed | tf_op | source)
XLA Modules:
  0.0 72.2 jit_solution(6424272644727841664)
XLA Ops:
  0.6 69.5 %banded_attention.1 = (f32[128,384]{1,0:T(8,128)}, f32[128,384]{1,0:T(8,128)}, f32[128,384]{1,0:T(8,128)}, f32[128,384]{1,0:T(8,128)}, f32[24,384]{1,0:T(8,128)}) custom-call(f32[128,384]{1,0:T(8,128)} %q_ref.1, f32[128,384]{1,0:T(8,128)} %k_ref.1, f32[128,384]{1,0:T(8,128)} %v_ref.1, s32[1,128]{1,0:T(1,128)} %bitcast.2, s32[16]{0:T(128)} %band_ref.1, ...), custom_call_target="tpu_custom_call" | custom-call | tf_op jit(solution)/shard_map/banded_attention/pallas_call | solution.py:491
  70.1 2.1 %hand_over.1 = (f32[128,384]{1,0:T(8,128)}, f32[128,384]{1,0:T(8,128)}, f32[128,384]{1,0:T(8,128)}, f32[128,384]{1,0:T(8,128)}, f32[24,384]{1,0:T(8,128)}) custom-call(f32[128,384]{1,0:T(8,128)} %get-tuple-element.15.refs_0_, f32[128,384]{1,0:T(8,128)} %get-tuple-element.16.refs_1_, f32[128,384]{1,0:T(8,128)} %get-tuple-element.17.refs_2_, ...), custom_call_target="tpu_custom_call" | custom-call | tf_op jit(solution)/shard_map/hand_over/pallas_call | solution.py:521

commit v3 on v2

--- a/solution.py
+++ b/solution.py
@@ -100,8 +100,7 @@
         return at((z + k) % NZ, x, y, core)
 
     peers = [pair(k) for k in (1, -1, 2, -2)]
-    peers += [along_y(k) for k in (1, 2, 3)] + [sibling]
-    peers += [along_x(k) for k in (1, 2, 3)]
+    peers += [along_y(1), along_y(3), sibling, along_x(1), along_x(3)]
     peers += [along_z(k) for k in range(1, NZ)]
     barrier = pltpu.get_barrier_semaphore()
     for peer in peers:
@@ -237,12 +236,12 @@
         return jnp.concatenate([column] * 8, axis=1) == row
 
     for h in range(2):
-        s_ref[...] = mul6(middle(qw, h * HD), window(kw, h * HD))
+        s_ref[h] = mul6(middle(qw, h * HD), window(kw, h * HD))
 
         def soften(i, carry, h=h):
             rows = pl.ds(pl.multiple_of(i * CHUNK, CHUNK), CHUNK)
             ok = allowed(i, i // (B // CHUNK), h)
-            scores = jnp.where(ok, s_ref[rows], -1e30)
+            scores = jnp.where(ok, s_ref[h, rows], -1e30)
             top = jnp.max(scores, axis=1, keepdims=True)
             e = jnp.exp(scores - top)
             total = jnp.sum(e, axis=1, keepdims=True)
@@ -275,6 +274,29 @@
             cotth[col * 384:(col + 1) * 384, row * B:(row + 1) * B] = hi
             cottm[col * 384:(col + 1) * 384, row * B:(row + 1) * B] = mid
 
+    relay(qw, q_sem)
+    do_t[...] = (dot_nt(wh[...], coth[...]) + dot_nt(wm[...], cotm[...])) + (
+        (dot_nt(wh[...], cotm[...]) + dot_nt(wm[...], coth[...]))
+        + (dot_nt(wh[...], cotl[...]) + dot_nt(wl[...], coth[...]))
+    )
+    dow[3] = do_t[:, :B]
+    dow[4] = do_t[:, B:]
+
+    def send_two(window, sem, base):
+        send(window.at[pl.ds(3, 2)], window.at[pl.ds(1, 2)], sem.at[base], pair(1))
+        send(window.at[pl.ds(3, 2)], window.at[pl.ds(5, 2)], sem.at[base + 1], pair(-1))
+
+    def relay_two(window, sem, base):
+        arrived(window.at[pl.ds(1, 2)], sem.at[base])
+        send(window.at[2], window.at[0], sem.at[base + 2], pair(1))
+        arrived(window.at[pl.ds(5, 2)], sem.at[base + 1])
+        send(window.at[5], window.at[7], sem.at[base + 3], pair(-1))
+
+    def arrived_two(window, sem, base):
+        arrived(window.at[0], sem.at[base + 2])
+        arrived(window.at[7], sem.at[base + 3])
+
+    send_two(dow, do_sem, 0)
     arrived_window(vw, v_sem)
 
     for h in range(2):
@@ -304,29 +326,15 @@
         send(mx.at[far, quad, thirds[0]], xfu.at[n], x_sem.at[n], along_x(1))
         send(mx.at[far, quad, thirds[1]], xfd.at[n], x_sem.at[2 + n], along_x(3))
 
-    relay(qw, q_sem)
-    do_t[...] = (dot_nt(wh[...], coth[...]) + dot_nt(wm[...], cotm[...])) + (
-        (dot_nt(wh[...], cotm[...]) + dot_nt(wm[...], coth[...]))
-        + (dot_nt(wh[...], cotl[...]) + dot_nt(wl[...], coth[...]))
-    )
-    dow[3] = do_t[:, :B]
-    dow[4] = do_t[:, B:]
-
-    def send_two(window, sem, base):
-        send(window.at[pl.ds(3, 2)], window.at[pl.ds(1, 2)], sem.at[base], pair(1))
-        send(window.at[pl.ds(3, 2)], window.at[pl.ds(5, 2)], sem.at[base + 1], pair(-1))
-
-    def relay_two(window, sem, base):
-        arrived(window.at[pl.ds(1, 2)], sem.at[base])
-        send(window.at[2], window.at[0], sem.at[base + 2], pair(1))
-        arrived(window.at[pl.ds(5, 2)], sem.at[base + 1])
-        send(window.at[5], window.at[7], sem.at[base + 3], pair(-1))
-
-    def arrived_two(window, sem, base):
-        arrived(window.at[0], sem.at[base + 2])
-        arrived(window.at[7], sem.at[base + 3])
-
-    send_two(dow, do_sem, 0)
+    for col in range(4):
+        part = mul_parts(
+            ath[...], atm[...],
+            wh[:, col * 384:(col + 1) * 384], wm[:, col * 384:(col + 1) * 384],
+        )
+        po[col % 2, (col // 2) * 2] = part[:B]
+        po[col % 2, (col // 2) * 2 + 1] = part[B:]
+    send(po.at[1 - core], por, po_sem, sibling)
+
     stats = col_ref[...].T
     deltas = [
         jnp.sum(do_t[h * HD:(h + 1) * HD] * att_t[h * HD:(h + 1) * HD], axis=0, keepdims=True)
@@ -347,17 +355,6 @@
         arrived(xfd.at[n], x_sem.at[2 + n])
         mx[down, quad, thirds[1]] = mx[down, quad, thirds[1]] + xfd[n]
         send(mx.at[down, quad], xr.at[1, n], x_sem.at[6 + n], along_x(3))
-    relay_two(dow, do_sem, 0)
-
-    for col in range(4):
-        part = mul_parts(
-            ath[...], atm[...],
-            wh[:, col * 384:(col + 1) * 384], wm[:, col * 384:(col + 1) * 384],
-        )
-        po[col % 2, (col // 2) * 2] = part[:B]
-        po[col % 2, (col // 2) * 2 + 1] = part[B:]
-    send(po.at[1 - core], por, po_sem, sibling)
-
     arrived(por, po_sem)
     for t in range(4):
         ps[t] = po[core, t] + por[t]
@@ -369,6 +366,13 @@
         gown[n, h] = jnp.where(yl == 0, result[:, :B], result[:, B:])
         gsend[n, h] = jnp.where(yl == 0, result[:, B:], result[:, :B])
         send(gsend.at[n, h], grecv.at[n, h], g_sem.at[n * 2 + h], partner)
+
+    def sum_half(n):
+        arrived(xr.at[0, n], x_sem.at[4 + n])
+        arrived(xr.at[1, n], x_sem.at[6 + n])
+        xs[quads[n]] = mx[x, quads[n]] + xr[0, n] + xr[1, n]
+        for k in ((4, 3, 5, 2), (6, 7, 1))[n]:
+            send(xs.at[(k + 6) % NZ], zr.at[k - 1], z_sem.at[k - 1], along_z(k))
 
     for h in range(2):
         delta_col = jnp.concatenate([rows[2 + h:3 + h], jnp.zeros((7, 2 * B), F32)], axis=0)
@@ -392,6 +396,7 @@
         result = (mul_window(ph[h], pm[h], window(kw, h * HD)) * SCALE).T[:HD]
         give(0, h, result)
         if h == 0:
+            relay_two(dow, do_sem, 0)
             arrived(pf.at[0], pr_sem.at[0])
             ps[up_y, 0:64] = ps[up_y, 0:64] + pf[0]
             send(ps.at[up_y], pr.at[0], pr_sem.at[2], along_y(1))
@@ -399,22 +404,17 @@
             ps[down_y, 64:128] = ps[down_y, 64:128] + pf[1]
             send(ps.at[down_y], pr.at[1], pr_sem.at[3], along_y(3))
 
-    def sum_half(n):
-        arrived(xr.at[0, n], x_sem.at[4 + n])
-        arrived(xr.at[1, n], x_sem.at[6 + n])
-        xs[quads[n]] = mx[x, quads[n]] + xr[0, n] + xr[1, n]
-        for k in ((4, 3, 5, 2), (6, 7, 1))[n]:
-            send(xs.at[(k + 6) % NZ], zr.at[k - 1], z_sem.at[k - 1], along_z(k))
-
     sum_half(0)
-
     arrived_window(qw, q_sem)
+    for h in range(2):
+        s_ref[h] = mul6(middle(kw, h * HD), window(qw, h * HD))
+
+    sum_half(1)
     arrived(stw.at[pl.ds(1, 2)], st_sem.at[0])
     arrived(stw.at[pl.ds(5, 2)], st_sem.at[1])
     arrived_two(stw, st_sem, 0)
     arrived_two(dow, do_sem, 0)
     for h in range(2):
-        s_ref[...] = mul6(middle(kw, h * HD), window(qw, h * HD))
         dp_ref[...] = mul6(middle(vw, h * HD), window(dow, h * HD))
         log_row = jnp.concatenate([stw[s, h:h + 1] for s in range(8)], axis=1)
         delta_row = jnp.concatenate([stw[s, 2 + h:3 + h] for s in range(8)], axis=1)
@@ -422,7 +422,7 @@
         def weigh_keys(i, carry, h=h, log_row=log_row, delta_row=delta_row):
             at_rows = pl.ds(pl.multiple_of(i * CHUNK, CHUNK), CHUNK)
             ok = allowed(i, i // (B // CHUNK), h)
-            probs = jnp.exp(jnp.where(ok, s_ref[at_rows] - log_row, -1e30))
+            probs = jnp.exp(jnp.where(ok, s_ref[h, at_rows] - log_row, -1e30))
             hi, mid = split2(probs)
             ph[h, at_rows] = hi
             pm[h, at_rows] = mid
@@ -433,8 +433,6 @@
         give(2, h, mul_window(ph[h], pm[h], window(dow, h * HD)).T[:HD])
         hi, mid = split2(dp_ref[...])
         give(1, h, mul_window(hi, mid, window(qw, h * HD)).T[:HD])
-        if h == 0:
-            sum_half(1)
 
     arrived(pr.at[0], pr_sem.at[2])
     arrived(pr.at[1], pr_sem.at[3])
@@ -504,7 +502,7 @@
             full(2, 4, B, 384), full(192, 1536), full(2 * B, B), full(4, 8, W8),
             half(2 * B, 1536), half(2 * B, 1536), half(2 * B, 1536), half(1536, 2 * B), half(1536, 2 * B),
             half(192, 1536), half(192, 1536), half(192, 1536),
-            full(2 * B, W8), full(2, 2 * B, W8), full(2 * B, W8),
+            full(2, 2 * B, W8), full(2, 2 * B, W8), full(2 * B, W8),
             half(2, 2 * B, W8), half(2, 2 * B, W8), full(2 * B, B),
             full(192, 2 * B), full(192, 2 * B), half(2 * B, 192), half(2 * B, 192),
             full(2, 4, B, 384), full(4, B, 384), full(4, B, 384), full(2, 64, 384), full(2, B, 384),

time: 72.4 us -> 67.5 us (0.932)
  Pallas kernels: 71.6 us -> 66.3 us
    pallas_call x1, Pallas kernels: 69.5 us -> 64.2 us  [shards(): pl.pallas_call(kernel, out_shape=(block, block, block, block, jax.ShapeDt...]
where the time goes in v3:
time: 67.5 us; the launch traced here: 67 us
  Pallas kernels  66.3 us (98%)
    pallas_call x1, Pallas kernels, shards(): pl.pallas_call(kernel, out_shape=(block, block, block, block, jax.ShapeDt...  64.2 us
    pallas_call x1, Pallas kernels, shards(): pl.pallas_call(hand_over, out_shape=[jax.ShapeDtypeStruct(r.shape, F32) f...  2.11 us

profile of v3, /device:TPU:8, one launch (start us, length us, event | category | flops | bytes accessed | tf_op | source)
XLA Modules:
  0.0 67.0 jit_solution(7336924068911272943)
XLA Ops:
  0.6 64.2 %banded_attention.1 = (f32[128,384]{1,0:T(8,128)}, f32[128,384]{1,0:T(8,128)}, f32[128,384]{1,0:T(8,128)}, f32[128,384]{1,0:T(8,128)}, f32[24,384]{1,0:T(8,128)}) custom-call(f32[128,384]{1,0:T(8,128)} %q_ref.1, f32[128,384]{1,0:T(8,128)} %k_ref.1, f32[128,384]{1,0:T(8,128)} %v_ref.1, s32[1,128]{1,0:T(1,128)} %bitcast.2, s32[16]{0:T(128)} %band_ref.1, ...), custom_call_target="tpu_custom_call" | custom-call | tf_op jit(solution)/shard_map/banded_attention/pallas_call | solution.py:489
  64.9 2.1 %hand_over.1 = (f32[128,384]{1,0:T(8,128)}, f32[128,384]{1,0:T(8,128)}, f32[128,384]{1,0:T(8,128)}, f32[128,384]{1,0:T(8,128)}, f32[24,384]{1,0:T(8,128)}) custom-call(f32[128,384]{1,0:T(8,128)} %get-tuple-element.15.refs_0_, f32[128,384]{1,0:T(8,128)} %get-tuple-element.16.refs_1_, f32[128,384]{1,0:T(8,128)} %get-tuple-element.17.refs_2_, ...), custom_call_target="tpu_custom_call" | custom-call | tf_op jit(solution)/shard_map/hand_over/pallas_call | solution.py:519

commit v4 on v3

--- a/solution.py
+++ b/solution.py
@@ -63,13 +63,14 @@
 
 
 def kernel(
-    q_ref, k_ref, v_ref, seg_ref, band_ref, w_ref, cot_ref,
-    out_ref, gq_ref, gk_ref, gv_ref, gw_ref,
+    q_in, k_in, v_in, seg_ref, band_ref, w_ref, cot_in,
+    out_hbm, gq_hbm, gk_hbm, gv_hbm, gw_hbm,
     tq, tkv, ks, vs, kw, vw, qs, qw, dow, stw, cotw, wv, lab_col, lab_row,
     coth, cotm, cotl, cotth, cottm, wh, wm, wl,
     s_ref, e_ref, dp_ref, ph, pm, col_ref, att_t, do_t, ath, atm,
     po, por, ps, pf, pr, mx, xfu, xfd, xr, xs, zr, gsum, yr, gown, gsend, grecv,
     ss, k_sem, v_sem, q_sem, do_sem, st_sem, cot_sem, y_sem, po_sem, pr_sem, x_sem, z_sem, g_sem, w_sem,
+    q_ref, k_ref, v_ref, in_sem, out_ref, gq_ref, gk_ref, gv_ref, gw_ref, out_sem,
 ):
     ctx = lax.axis_index("ctx")
     head = lax.axis_index("head")
@@ -106,6 +107,14 @@
     for peer in peers:
         pl.semaphore_signal(barrier, inc=1, device_id=peer, device_id_type=MESH)
 
+    inputs = [
+        pltpu.make_async_copy(src, dst, in_sem.at[n])
+        for n, (src, dst) in enumerate(
+            ((k_in, k_ref), (v_in, v_ref), (q_in, q_ref), (cot_in, cotw.at[yl, head]))
+        )
+    ]
+    for copy in inputs:
+        copy.start()
     w_copy = pltpu.make_async_copy(
         w_ref.at[pl.ds(pl.multiple_of(yl * 192, 8), 192)], wv, w_sem
     )
@@ -132,15 +141,18 @@
 
     mine = pl.ds(pl.multiple_of(yl * 192, 8), 192)
     rest = pl.ds(pl.multiple_of(other * 192, 8), 192)
+    inputs[0].wait()
     tkv[0] = k_ref[...].T
     label = jnp.broadcast_to((seg_ref[...] + 1).astype(F32), (8, B))
     ks[0:192] = tkv[0, rest]
     ks[192:200] = label
     kw[own, 0:192] = tkv[0, mine]
     kw[own, 192:200] = label
+    inputs[1].wait()
     tkv[1] = v_ref[...].T
     vs[...] = tkv[1, rest]
     vw[own] = tkv[1, mine]
+    inputs[2].wait()
     tq[...] = (q_ref[...] * SCALE).T
     qs[...] = tq[rest]
     qw[own] = tq[mine]
@@ -166,7 +178,7 @@
     send_block(kw, k_sem, own, yl)
     send_block(vw, v_sem, own, yl)
     send(qs, qw.at[own], q_sem.at[own], partner)
-    cotw[yl, head] = cot_ref[...]
+    inputs[3].wait()
     arrived(kw.at[theirs], k_sem.at[theirs])
     send_block(kw, k_sem, theirs, other)
     arrived(vw.at[theirs], v_sem.at[theirs])
@@ -434,9 +446,16 @@
         hi, mid = split2(dp_ref[...])
         give(1, h, mul_window(hi, mid, window(qw, h * HD)).T[:HD])
 
+    written = []
+
+    def write(n, src, dst):
+        written.append(pltpu.make_async_copy(src, dst, out_sem.at[n]))
+        written[-1].start()
+
     arrived(pr.at[0], pr_sem.at[2])
     arrived(pr.at[1], pr_sem.at[3])
     out_ref[...] = ps[y] + pr[0] + pr[1]
+    write(0, out_ref, out_hbm)
 
     total = xs[6]
     for k in range(1, NZ):
@@ -445,12 +464,14 @@
     gsum[...] = total
     send(gsum, yr, y_sem, partner)
 
+    homes = gq_hbm, gk_hbm, gv_hbm
     for n, ref in enumerate((gq_ref, gk_ref, gv_ref)):
         for h in range(2):
             arrived(grecv.at[n, h], g_sem.at[n * 2 + h])
         lower = [jnp.where(yl == 0, gown[n, h], grecv[n, h]) for h in range(2)]
         upper = [jnp.where(yl == 0, grecv[n, h], gown[n, h]) for h in range(2)]
         ref[...] = jnp.concatenate(lower + upper, axis=0).T
+        write(1 + n, ref, homes[n])
 
     arrived(yr, y_sem)
     lower = jnp.where(yl == 0, gsum[...], yr[...])
@@ -461,10 +482,13 @@
         last = part[48:72]
         pieces.append(jnp.where(yl == 0, last[:, :64], last[:, 64:]))
     gw_ref[...] = jnp.concatenate(pieces, axis=1)
+    write(4, gw_ref, gw_hbm)
 
     assert len(pending) == SENDS
     for copy in pending:
         copy.wait_send()
+    for copy in written:
+        copy.wait()
 
 
 SENDS = 65
@@ -477,6 +501,7 @@
 
 def shards(query, key, value, segment, band, out_weight, cotangent):
     vmem = pl.BlockSpec(memory_space=pltpu.VMEM)
+    anywhere = pl.BlockSpec(memory_space=pl.ANY)
 
     def full(*shape):
         return pltpu.VMEM(shape, F32)
@@ -490,12 +515,11 @@
         kernel,
         out_shape=(block, block, block, block, jax.ShapeDtypeStruct((24, 384), F32)),
         in_specs=[
-            vmem, vmem, vmem, vmem,
+            anywhere, anywhere, anywhere, vmem,
             pl.BlockSpec(memory_space=pltpu.SMEM),
-            pl.BlockSpec(memory_space=pl.ANY),
-            vmem,
+            anywhere, anywhere,
         ],
-        out_specs=[vmem] * 5,
+        out_specs=[anywhere] * 5,
         scratch_shapes=[
             full(384, B), full(2, 384, B), full(200, B), full(192, B), full(8, 200, B), full(8, 192, B),
             full(192, B), full(8, 192, B), full(8, 192, B), full(8, 8, B),
@@ -510,6 +534,8 @@
             full(72, B), full(72, B), full(3, 2, HD, B), full(3, 2, HD, B), full(3, 2, HD, B),
             dma((SENDS,)), dma((8,)), dma((8,)), dma((8,)), dma((4,)), dma((4,)), dma((8, 2)), dma,
             dma, dma((4,)), dma((8,)), dma((NZ - 1,)), dma((6,)), dma,
+            full(B, 384), full(B, 384), full(B, 384), dma((4,)),
+            full(B, 384), full(B, 384), full(B, 384), full(B, 384), full(24, 384), dma((5,)),
         ],
         compiler_params=pltpu.CompilerParams(
             collective_id=0, has_side_effects=True, vmem_limit_bytes=58 * 2**20

time: 67.5 us -> 66.7 us (0.988)
  Pallas kernels: 66.3 us -> 65.6 us
    pallas_call x1, Pallas kernels: 64.2 us -> 63.5 us  [shards(): pl.pallas_call(kernel, out_shape=(block, block, block, block, jax.ShapeDt...]
where the time goes in v4:
time: 66.7 us; the launch traced here: 66.2 us
  Pallas kernels  65.6 us (98%)
    pallas_call x1, Pallas kernels, shards(): pl.pallas_call(kernel, out_shape=(block, block, block, block, jax.ShapeDt...  63.5 us
    pallas_call x1, Pallas kernels, shards(): pl.pallas_call(hand_over, out_shape=[jax.ShapeDtypeStruct(r.shape, F32) f...  2.11 us

profile of v4, /device:TPU:8, one launch (start us, length us, event | category | flops | bytes accessed | tf_op | source)
XLA Modules:
  0.0 66.2 jit_solution(15441684689654182531)
XLA Ops:
  0.6 63.5 %banded_attention.1 = (f32[128,384]{1,0:T(8,128)}, f32[128,384]{1,0:T(8,128)}, f32[128,384]{1,0:T(8,128)}, f32[128,384]{1,0:T(8,128)}, f32[24,384]{1,0:T(8,128)}) custom-call(f32[128,384]{1,0:T(8,128)} %q_in.1, f32[128,384]{1,0:T(8,128)} %k_in.1, f32[128,384]{1,0:T(8,128)} %v_in.1, s32[1,128]{1,0:T(1,128)} %bitcast.2, s32[16]{0:T(128)} %band_ref.1, ...), custom_call_target="tpu_custom_call" | custom-call | tf_op jit(solution)/shard_map/banded_attention/pallas_call | solution.py:514
  64.1 2.1 %hand_over.1 = (f32[128,384]{1,0:T(8,128)}, f32[128,384]{1,0:T(8,128)}, f32[128,384]{1,0:T(8,128)}, f32[128,384]{1,0:T(8,128)}, f32[24,384]{1,0:T(8,128)}) custom-call(f32[128,384]{1,0:T(8,128)} %get-tuple-element.15.refs_0_, f32[128,384]{1,0:T(8,128)} %get-tuple-element.16.refs_1_, f32[128,384]{1,0:T(8,128)} %get-tuple-element.17.refs_2_, ...), custom_call_target="tpu_custom_call" | custom-call | tf_op jit(solution)/shard_map/hand_over/pallas_call | solution.py:545
